TPU v7x, 32 devices: a whole 2x2x4 slice. The times are simulated.
32 devices in a mesh: lat: 8 (over z, x), lon: 4 (over y, core).
Axes of the slice: x: 2, y: 2, z: 4, core: 2. Of those that a mesh axis runs over, the one named last changes fastest.
Arguments:
- tracer: float32 [32, 192, 1152], P(None, 'lat', 'lon'), may hold values from -6 to 6
- wind_u: float32 [32, 192, 1152], P(None, 'lat', 'lon'), may hold values from -2.5 to 2.5
- wind_v: float32 [32, 192, 1152], P(None, 'lat', 'lon'), may hold values from -2.5 to 2.5
- ocean_temp: float32 [4, 256, 3584], P(None, 'lat', 'lon'), may hold values from -6 to 6
- land_mask: int32 [256, 3584], P('lat', 'lon'), may hold values 0 or 1
- remap_rows: int32 [256, 3584], P('lat', 'lon'), may hold values from 0 to 191, as said below
- remap_cols: int32 [256, 3584], P('lat', 'lon'), may hold values from 0 to 1151, as said below
- polar_rows: int32 [24], replicated, may hold values from 0 to 191, as said below
Outputs:
- tracer_out: float32 [32, 192, 1152], P(None, 'lat', 'lon')
- ocean_out: float32 [4, 256, 3584], P(None, 'lat', 'lon')
Inputs may be any that keep to these rules, and one draw needn't show every extreme that they name: `remap_rows`: for an ocean cell in row block b of 32 rows, an atmosphere row from b * 24 - 1 to (b + 1) * 24, within the grid. `remap_cols`: for an ocean cell in column block c of 896 columns, an atmosphere column from c * 288 - 1 to (c + 1) * 288, modulo 1152. `polar_rows`: distinct rows, each among the 24 rows nearest either pole.
All inputs are finite; a program needn't handle non-finite values. No bound on the sum of `land_mask` on one device may be relied on, other than what follows from the above.
Results may differ from a plain program's by a relative error of at most 0.0001.
Values sent between devices are 32-bit elements; how exact they have to be, the bound alone decides.
A program may use at most 128 MiB of HBM per device.

v0:
```python
import math

import jax
import jax.numpy as jnp
from jax import lax
from jax.sharding import PartitionSpec as P

STEPS = 2
OSTEPS = 2


advect_coef = 0.2
diffuse_coef = 0.1
flux_coef = 0.25
ocean_diffuse = 0.15
vertical_mix = 0.2
highest = lax.Precision.HIGHEST


def padded_2(shard, sides, width, wrap):
    for axis, dim in sides:
        count, length = (lax.axis_size(axis), shard.shape[dim])
        up = [(i, (i + 1) % count) for i in range(count if wrap else count - 1)]
        down = [(j, i) for i, j in up]
        last = lax.slice_in_dim(shard, length - width, length, axis=dim)
        first = lax.slice_in_dim(shard, 0, width, axis=dim)
        before = lax.ppermute(last, axis, up)
        after = lax.ppermute(first, axis, down)
        shard = jnp.concatenate([before, shard, after], axis=dim)
    return shard


def damp_table(row_index, polar_rows, wave_numbers, lat_total, band_rows, lon_total):
    latitude_cos = jnp.sin(math.pi * (row_index.astype(jnp.float32) + 0.5) / lat_total)
    ratio = latitude_cos / math.sin(math.pi * band_rows / lat_total)
    wave_sine = jnp.sin(math.pi * wave_numbers / lon_total)
    safe_sine = jnp.where(wave_numbers > 0.5, wave_sine, 1.0)
    damping = jnp.where(
        wave_numbers[None, :] > 0.5, jnp.minimum(1.0, ratio[:, None] / safe_sine[None, :]), 1.0
    )
    listed = jnp.any(row_index[:, None] == polar_rows[None, :], axis=1)
    return jnp.where(listed[:, None], damping, 1.0)


def make_basis(lon_total):
    half_circle = lon_total // 2
    points = jnp.arange(lon_total, dtype=jnp.int32)
    cos_waves = jnp.arange(half_circle + 1, dtype=jnp.int32)
    sin_waves = jnp.arange(1, half_circle, dtype=jnp.int32)
    cos_phase = points[:, None] * cos_waves[None, :] % lon_total
    sin_phase = points[:, None] * sin_waves[None, :] % lon_total
    basis = jnp.concatenate(
        [
            jnp.cos(2.0 * math.pi * cos_phase.astype(jnp.float32) / lon_total),
            jnp.sin(2.0 * math.pi * sin_phase.astype(jnp.float32) / lon_total),
        ],
        axis=1,
    )
    waves_all = jnp.concatenate([cos_waves, sin_waves])
    wave_numbers = waves_all.astype(jnp.float32)
    weight = jnp.where(
        (waves_all == 0) | (waves_all == half_circle), 1.0 / lon_total, 2.0 / lon_total
    )
    return (basis, wave_numbers, weight)


def rim(field):
    wider = padded_2(field, (("lat", 1),), 1, False)
    return padded_2(wider, (("lon", 2),), 1, True)


def atmos_step(tracer_now, wind_u, wind_v):
    padded = rim(tracer_now)
    east_side = padded[:, 1:-1, 2:]
    west_side = padded[:, 1:-1, :-2]
    north_side = padded[:, 2:, 1:-1]
    south_side = padded[:, :-2, 1:-1]
    advect = wind_u * (east_side - west_side) + wind_v * (north_side - south_side)
    spread_sum = east_side + west_side + north_side + south_side - 4.0 * tracer_now
    return tracer_now - advect_coef * advect + diffuse_coef * spread_sum


def back_project(scaled, target_basis):
    return lax.dot_general(
        scaled,
        target_basis,
        (((1,), (1,)), ((), ())),
        precision=highest,
        preferred_element_type=jnp.float32,
    )


def ocean_step(temp, sea, air_temp, air_speed):
    top_level = temp[0] + sea * flux_coef * air_speed * (air_temp - temp[0])
    temp = jnp.concatenate([top_level[None], temp[1:]], axis=0)
    padded = rim(jnp.concatenate([temp, sea[None]], axis=0))
    level_count = temp.shape[0]
    temp_rim = padded[:level_count]
    sea_rim = padded[level_count]
    lateral = sea * (
        sea_rim[1:-1, 2:] * (temp_rim[:, 1:-1, 2:] - temp)
        + sea_rim[1:-1, :-2] * (temp_rim[:, 1:-1, :-2] - temp)
        + sea_rim[2:, 1:-1] * (temp_rim[:, 2:, 1:-1] - temp)
        + sea_rim[:-2, 1:-1] * (temp_rim[:, :-2, 1:-1] - temp)
    )
    temp = temp + ocean_diffuse * lateral
    upper = jnp.concatenate([temp[:1], temp[:-1]], axis=0)
    lower = jnp.concatenate([temp[1:], temp[-1:]], axis=0)
    return temp + vertical_mix * sea * (upper + lower - 2.0 * temp)


def per_device(tracer, wind_u, wind_v, ocean_temp, land_mask, remap_rows, remap_cols, polar_rows):
    levels, row_count, lon_local = tracer.shape
    lat_devices = lax.axis_size("lat")
    lon_devices = lax.axis_size("lon")
    lat_total = row_count * lat_devices
    lon_total = lon_local * lon_devices
    band_devices = lat_devices // 8
    band_rows = band_devices * row_count
    lat_place = lax.axis_index("lat")
    lon_place = lax.axis_index("lon")
    basis, wave_numbers, weight = make_basis(lon_total)
    own_basis = lax.dynamic_slice_in_dim(basis, lon_place * lon_local, lon_local, 0)
    own_rows = lat_place * row_count + jnp.arange(row_count, dtype=jnp.int32)
    line_count = levels * row_count
    tracer_now = tracer
    for step_index in range(STEPS):
        tracer_now = atmos_step(tracer_now, wind_u, wind_v)
        row_weights = (
            damp_table(own_rows, polar_rows, wave_numbers, lat_total, band_rows, lon_total)
            * weight[None, :]
        )
        lines = tracer_now.reshape(line_count, lon_local)
        coeffs = jnp.dot(
            lax.all_gather(lines, "lon", axis=1, tiled=True),
            basis,
            precision=highest,
            preferred_element_type=jnp.float32,
        )
        scaled = (coeffs.reshape(levels, row_count, lon_total) * row_weights[None]).reshape(
            line_count, lon_total
        )
        tracer_now = back_project(scaled, own_basis).reshape(levels, row_count, lon_local)
    bottom = jnp.stack(
        [tracer_now[levels - 1], jnp.abs(wind_u[levels - 1]) + jnp.abs(wind_v[levels - 1]) + 0.5]
    )
    bottom_rim = rim(bottom)
    local_row = remap_rows - lat_place * row_count + 1
    local_col = (remap_cols - lon_place * lon_local + 1) % lon_total
    flat_index = local_row * (lon_local + 2) + local_col
    picked = jnp.take(bottom_rim.reshape(2, -1), flat_index, axis=1)
    air_temp = picked[0]
    air_speed = picked[1]
    sea = land_mask.astype(jnp.float32)
    temp = ocean_temp
    for step_index in range(OSTEPS):
        temp = ocean_step(temp, sea, air_temp, air_speed)
    return (tracer_now, temp)


def solution(mesh):
    in_specs = (
        P(None, "lat", "lon"),
        P(None, "lat", "lon"),
        P(None, "lat", "lon"),
        P(None, "lat", "lon"),
        P("lat", "lon"),
        P("lat", "lon"),
        P("lat", "lon"),
        P(),
    )
    out_specs = (P(None, "lat", "lon"), P(None, "lat", "lon"))
    return jax.shard_map(
        per_device, mesh=mesh, in_specs=in_specs, out_specs=out_specs, check_vma=False
    )
```

profile of v0, /device:TPU:0, one launch (start us, length us, event | category | flops | bytes accessed | tf_op | source)
XLA Modules:
  0.0 355.5 jit_solution(13403060972353101339)
XLA Ops:
  8.5 5.0 %collective-permute-start = (f32[32,1,288]{2,1,0:T(1,128)S(1)}, f32[32,1,288]{2,1,0:T(1,128)S(1)}, u32[]{:S(2)}, u32[]{:S(2)}) collective-permute-start(f32[32,1,288]{2,1,0:T(1,128)S(1)} %get-tuple-element.12), channel_id=1, source_target_pairs={{0,4},{4,8},{8,12},{12,16},{16,20},{20,24},{24,28},{1,5},{5,9},{9,... | collective-permute-start | bytes 110600 | tf_op jit(solution)/shard_map/ppermute | solution.py:27
  15.2 4.3 %collective-permute-done.1 = f32[32,1,288]{2,1,0:T(1,128)S(1)} collective-permute-done((f32[32,1,288]{2,1,0:T(1,128)S(1)}, f32[32,1,288]{2,1,0:T(1,128)S(1)}, u32[]{:S(2)}, u32[]{:S(2)}) %collective-permute-start.1) | collective-permute-done | bytes 36896 | tf_op jit(solution)/shard_map/ppermute | solution.py:28
  21.5 10.8 %collective-permute-done.2 = f32[32,26,1]{2,1,0:T(8,128)S(1)} collective-permute-done((f32[32,26,1]{2,1,0:T(8,128)S(1)}, f32[32,26,1]{2,1,0:T(8,128)S(1)}, u32[]{:S(2)}, u32[]{:S(2)}) %collective-permute-start.2) | collective-permute-done | bytes 3360 | tf_op jit(solution)/shard_map/ppermute | solution.py:28
  32.3 3.0 collective-permute-done.3
  35.2 2.8 multiply_add_fusion.1
  40.1 11.0 %fusion.2 = f32[1152,577]{1,0:T(8,128)S(1)} fusion(), kind=kLoop, calls=%fused_computation.10 | loop fusion | flops 5982336 | bytes 2658816 | tf_op jit(solution)/shard_map/cos | solution.py:54
  51.2 12.8 %fusion.5 = f32[1152,575]{1,0:T(8,128)} fusion(s32[575]{0:T(1024)S(1)} %iota_add_fusion), kind=kLoop, calls=%fused_computation.13 | loop fusion | flops 5961600 | bytes 2651900 | tf_op jit(solution)/shard_map/sin | solution.py:55
  64.0 6.4 %all-gather.3.cloned.1.call-done = f32[768,1152]{0,1:T(8,128)} async-done(((f32[768,288]{0,1:T(8,128)}), f32[768,1152]{0,1:T(8,128)}) %all-gather.3.cloned.1.call-update) | async-done | bytes 3538960 | tf_op jit(solution)/shard_map/all_gather | solution.py:135
  70.5 21.0 %bitcast_multiply_fusion.1 = f32[768,1152]{1,0:T(8,128)S(1)} fusion(f32[768,1152]{0,1:T(8,128)} %all-gather.3.cloned.1.call-done, f32[1152,575]{1,0:T(8,128)} %fusion.5, f32[1152,577]{1,0:T(8,128)S(1)} %fusion.2, f32[24,1152]{1,0:T(8,128)S(1)} %fusion.87), kind=kOutput, calls=%fused_computation.5 | convolution fusion | flops 12232802304 | bytes 12496896 | tf_op jit(solution)/shard_map/dot_general | solution.py:134
  91.4 6.2 %fusion.13 = f32[32,24,288]{2,1,0:T(8,128)S(1)} fusion(f32[32,24,1152]{2,1,0:T(8,128)S(1)} %bitcast.57, s32[]{:T(128)S(6)} %select_n.72, f32[1152,577]{1,0:T(8,128)S(1)} %fusion.2, f32[1152,575]{1,0:T(8,128)S(1)} %copy-done), kind=kOutput, calls=%fused_computation.23 | convolution fusion | flops 3057979392 | bytes 9732100 | tf_op jit(solution)/shard_map/dot_general | solution.py:84
  97.8 3.5 collective-permute-start.4
  103.0 4.3 %collective-permute-done.5 = f32[32,1,288]{2,1,0:T(1,128)S(1)} collective-permute-done((f32[32,1,288]{2,1,0:T(1,128)S(1)}, f32[32,1,288]{2,1,0:T(1,128)S(1)}, u32[]{:S(2)}, u32[]{:S(2)}) %collective-permute-start.5) | collective-permute-done | bytes 36896 | tf_op jit(solution)/shard_map/ppermute | solution.py:28
  108.3 11.4 %collective-permute-done.6 = f32[32,26,1]{2,1,0:T(8,128)S(1)} collective-permute-done((f32[32,26,1]{2,1,0:T(8,128)S(1)}, f32[32,26,1]{2,1,0:T(8,128)S(1)}, u32[]{:S(2)}, u32[]{:S(2)}) %collective-permute-start.6) | collective-permute-done | bytes 3360 | tf_op jit(solution)/shard_map/ppermute | solution.py:28
  121.0 2.5 multiply_add_fusion
  123.5 2.5 copy.31
  129.0 28.9 %all-gather.5.cloned.1.call-done = f32[768,1152]{0,1:T(8,128)} async-done(((f32[768,288]{0,1:T(8,128)}), f32[768,1152]{0,1:T(8,128)}) %all-gather.5.cloned.1.call-update) | async-done | bytes 3538960 | tf_op jit(solution)/shard_map/all_gather | solution.py:135
  157.9 21.2 %bitcast_multiply_fusion = f32[768,1152]{1,0:T(8,128)S(1)} fusion(f32[768,1152]{0,1:T(8,128)} %all-gather.5.cloned.1.call-done, f32[1152,575]{1,0:T(8,128)} %fusion.5, f32[1152,577]{1,0:T(8,128)S(1)} %fusion.2, f32[24,1152]{1,0:T(8,128)S(1)} %fusion.87), kind=kOutput, calls=%fused_computation.4 | convolution fusion | flops 12232802304 | bytes 12496896 | tf_op jit(solution)/shard_map/dot_general | solution.py:134
  179.1 4.1 %fusion.90 = f32[768,288]{0,1:T(8,128)S(1)} fusion(f32[768,1152]{1,0:T(8,128)S(1)} %bitcast_multiply_fusion, s32[]{:T(128)S(6)} %select_n.72, f32[1152,577]{1,0:T(8,128)S(1)} %fusion.2, f32[1152,575]{1,0:T(8,128)S(1)} %copy-done.1), kind=kOutput, calls=%fused_computation.184 | convolution fusion | flops 3057979392 | bytes 9732100 | tf_op jit(solution)/shard_map/dot_general | solution.py:84
  184.4 3.5 collective-permute-start.8
  189.4 11.5 %collective-permute-done.8 = f32[2,1,288]{1,2,0:T(8,128)S(1)} collective-permute-done((f32[2,1,288]{1,2,0:T(8,128)S(1)}, f32[2,1,288]{1,2,0:T(8,128)S(1)}, u32[]{:S(2)}, u32[]{:S(2)}) %collective-permute-start.8) | collective-permute-done | bytes 2336 | tf_op jit(solution)/shard_map/ppermute | solution.py:27
  201.3 1.9 collective-permute-start.11
  205.1 2.7 copy.39
  207.8 97.5 %gather_fusion = f32[28672,2]{1,0:T(8,128)} fusion(f32[2,7540]{0,1:T(8,128)} %copy.39, s32[28672]{0:T(1024)S(1)} %broadcast_clamp_fusion), kind=kCustom, calls=%fused_computation | custom fusion | bytes 573440 | tf_op jit(solution)/shard_map/jit(_take)/gather | solution.py:151
  305.3 9.0 %copy.40 = f32[32,896,2]{1,0,2:T(8,128)S(1)} copy(f32[32,896,2]{2,1,0:T(8,128)} %bitcast.56) | data formatting | bytes 458752 | tf_op jit(solution)/shard_map/jit(_take)/gather | solution.py:151
  314.4 4.4 %collective-permute-start.12 = (f32[5,1,896]{2,1,0:T(1,128)S(1)}, f32[5,1,896]{2,1,0:T(1,128)S(1)}, u32[]{:S(2)}, u32[]{:S(2)}) collective-permute-start(f32[5,1,896]{2,1,0:T(1,128)S(1)} %get-tuple-element.21), channel_id=1, source_target_pairs={{0,4},{4,8},{8,12},{12,16},{16,20},{20,24},{24,28},{1,5},{5,9},{9,... | collective-permute-start | bytes 53768 | tf_op jit(solution)/shard_map/ppermute | solution.py:27
  320.3 4.4 %collective-permute-done.13 = f32[5,1,896]{2,1,0:T(1,128)S(1)} collective-permute-done((f32[5,1,896]{2,1,0:T(1,128)S(1)}, f32[5,1,896]{2,1,0:T(1,128)S(1)}, u32[]{:S(2)}, u32[]{:S(2)}) %collective-permute-start.13) | collective-permute-done | bytes 17952 | tf_op jit(solution)/shard_map/ppermute | solution.py:28
  325.0 1.7 collective-permute-start.15
  326.7 2.6 collective-permute-done.14
  330.9 5.0 %collective-permute-start.16 = (f32[5,1,896]{2,1,0:T(1,128)S(1)}, f32[5,1,896]{2,1,0:T(1,128)S(1)}, u32[]{:S(2)}, u32[]{:S(2)}) collective-permute-start(f32[5,1,896]{2,1,0:T(1,128)S(1)} %get-tuple-element.19), channel_id=1, source_target_pairs={{0,4},{4,8},{8,12},{12,16},{16,20},{20,24},{24,28},{1,5},{5,9},{9,... | collective-permute-start | bytes 53768 | tf_op jit(solution)/shard_map/ppermute | solution.py:27
  337.3 4.2 %collective-permute-done.17 = f32[5,1,896]{2,1,0:T(1,128)S(1)} collective-permute-done((f32[5,1,896]{2,1,0:T(1,128)S(1)}, f32[5,1,896]{2,1,0:T(1,128)S(1)}, u32[]{:S(2)}, u32[]{:S(2)}) %collective-permute-start.17) | collective-permute-done | bytes 17952 | tf_op jit(solution)/shard_map/ppermute | solution.py:28
  341.8 1.7 collective-permute-start.19
  344.9 1.5 collective-permute-done.18
  (108 shorter events, 27.6 us)
Async XLA Ops:
  7.2 63.3 %all-gather.3.cloned.1.call-start = ((), (), s32[]{:S(2)}) async-start(), calls=%async_computation | async-start | bytes 4423680 | tf_op jit(solution)/shard_map/all_gather | solution.py:135
  7.2 28.0 %copy-start.3 = (f32[32,24,288]{2,1,0:T(8,128)S(1)}, f32[32,24,288]{2,1,0:T(8,128)}, u32[]{:S(2)}) copy-start(f32[32,24,288]{2,1,0:T(8,128)} %param.9) | copy-start | bytes 2654212
  8.5 26.7 %copy-start.2 = (f32[32,24,288]{2,1,0:T(8,128)S(1)}, f32[32,24,288]{2,1,0:T(8,128)}, u32[]{:S(2)}) copy-start(f32[32,24,288]{2,1,0:T(8,128)} %param.8) | copy-start | bytes 2654212
  8.5 6.7 %collective-permute-start = (f32[32,1,288]{2,1,0:T(1,128)S(1)}, f32[32,1,288]{2,1,0:T(1,128)S(1)}, u32[]{:S(2)}, u32[]{:S(2)}) collective-permute-start(f32[32,1,288]{2,1,0:T(1,128)S(1)} %get-tuple-element.12), channel_id=1, source_target_pairs={{0,4},{4,8},{8,12},{12,16},{16,20},{20,24},{24,28},{1,5},{5,9},{9,... | collective-permute-start | bytes 110600 | tf_op jit(solution)/shard_map/ppermute | solution.py:27
  13.5 6.0 %collective-permute-start.1 = (f32[32,1,288]{2,1,0:T(1,128)S(1)}, f32[32,1,288]{2,1,0:T(1,128)S(1)}, u32[]{:S(2)}, u32[]{:S(2)}) collective-permute-start(f32[32,1,288]{2,1,0:T(1,128)S(1)} %get-tuple-element.13), channel_id=1, source_target_pairs={{4,0},{8,4},{12,8},{16,12},{20,16},{24,20},{28,24},{5,1},{9,5},{13... | collective-permute-start | bytes 110600 | tf_op jit(solution)/shard_map/ppermute | solution.py:28
  20.9 11.4 %collective-permute-start.2 = (f32[32,26,1]{2,1,0:T(8,128)S(1)}, f32[32,26,1]{2,1,0:T(8,128)S(1)}, u32[]{:S(2)}, u32[]{:S(2)}) collective-permute-start(f32[32,26,1]{2,1,0:T(8,128)S(1)} %get-tuple-element.9), channel_id=1, source_target_pairs={{1,0},{2,1},{3,2},{0,3},{5,4},{6,5},{7,6},{4,7},{9,8},{10,9},{11,1... | collective-permute-start | bytes 9992 | tf_op jit(solution)/shard_map/ppermute | solution.py:28
  21.0 14.3 %collective-permute-start.3 = (f32[32,26,1]{2,1,0:T(8,128)S(1)}, f32[32,26,1]{2,1,0:T(8,128)S(1)}, u32[]{:S(2)}, u32[]{:S(2)}) collective-permute-start(f32[32,26,1]{2,1,0:T(8,128)S(1)} %get-tuple-element.8), channel_id=1, source_target_pairs={{0,1},{1,2},{2,3},{3,0},{4,5},{5,6},{6,7},{7,4},{8,9},{9,10},{10,1... | collective-permute-start | bytes 9992 | tf_op jit(solution)/shard_map/ppermute | solution.py:27
  39.3 118.6 %all-gather.5.cloned.1.call-start = ((), (), s32[]{:S(2)}) async-start(), calls=%async_computation.1 | async-start | bytes 4423680 | tf_op jit(solution)/shard_map/all_gather | solution.py:135
  70.5 21.0 %copy-start = (f32[1152,575]{1,0:T(8,128)S(1)}, f32[1152,575]{1,0:T(8,128)}, u32[]{:S(2)}) copy-start(f32[1152,575]{1,0:T(8,128)} %fusion.5) | copy-start | bytes 7948804
  97.7 23.3 %copy-start.5 = (f32[32,24,288]{2,1,0:T(8,128)S(1)}, f32[32,24,288]{2,1,0:T(8,128)}, u32[]{:S(2)}) copy-start(f32[32,24,288]{2,1,0:T(8,128)} %param.10) | copy-start | bytes 2654212
  97.8 23.2 %copy-start.4 = (f32[32,24,288]{2,1,0:T(8,128)S(1)}, f32[32,24,288]{2,1,0:T(8,128)}, u32[]{:S(2)}) copy-start(f32[32,24,288]{2,1,0:T(8,128)} %param.9) | copy-start | bytes 2654212
  97.8 5.2 %collective-permute-start.4 = (f32[32,1,288]{2,1,0:T(1,128)S(1)}, f32[32,1,288]{2,1,0:T(1,128)S(1)}, u32[]{:S(2)}, u32[]{:S(2)}) collective-permute-start(f32[32,1,288]{2,1,0:T(1,128)S(1)} %get-tuple-element.10), channel_id=1, source_target_pairs={{0,4},{4,8},{8,12},{12,16},{16,20},{20,24},{24,28},{1,5},{5,9},{9,... | collective-permute-start | bytes 110600 | tf_op jit(solution)/shard_map/ppermute | solution.py:27
  101.3 6.0 %collective-permute-start.5 = (f32[32,1,288]{2,1,0:T(1,128)S(1)}, f32[32,1,288]{2,1,0:T(1,128)S(1)}, u32[]{:S(2)}, u32[]{:S(2)}) collective-permute-start(f32[32,1,288]{2,1,0:T(1,128)S(1)} %get-tuple-element.11), channel_id=1, source_target_pairs={{4,0},{8,4},{12,8},{16,12},{20,16},{24,20},{28,24},{5,1},{9,5},{13... | collective-permute-start | bytes 110600 | tf_op jit(solution)/shard_map/ppermute | solution.py:28
  107.6 12.1 %collective-permute-start.6 = (f32[32,26,1]{2,1,0:T(8,128)S(1)}, f32[32,26,1]{2,1,0:T(8,128)S(1)}, u32[]{:S(2)}, u32[]{:S(2)}) collective-permute-start(f32[32,26,1]{2,1,0:T(8,128)S(1)} %get-tuple-element.7), channel_id=1, source_target_pairs={{1,0},{2,1},{3,2},{0,3},{5,4},{6,5},{7,6},{4,7},{9,8},{10,9},{11,1... | collective-permute-start | bytes 9992 | tf_op jit(solution)/shard_map/ppermute | solution.py:28
  107.6 13.3 %collective-permute-start.7 = (f32[32,26,1]{2,1,0:T(8,128)S(1)}, f32[32,26,1]{2,1,0:T(8,128)S(1)}, u32[]{:S(2)}, u32[]{:S(2)}) collective-permute-start(f32[32,26,1]{2,1,0:T(8,128)S(1)} %get-tuple-element.6), channel_id=1, source_target_pairs={{0,1},{1,2},{2,3},{3,0},{4,5},{5,6},{6,7},{7,4},{8,9},{9,10},{10,1... | collective-permute-start | bytes 9992 | tf_op jit(solution)/shard_map/ppermute | solution.py:27
  123.5 2.7 slice-start.1
  157.9 21.2 %copy-start.1 = (f32[1152,575]{1,0:T(8,128)S(1)}, f32[1152,575]{1,0:T(8,128)}, u32[]{:S(2)}) copy-start(f32[1152,575]{1,0:T(8,128)} %fusion.5) | copy-start | bytes 7948804
  184.2 19.0 %copy-start.8 = (s32[32,896]{1,0:T(8,128)S(1)}, s32[32,896]{1,0:T(8,128)}, u32[]{:S(2)}) copy-start(s32[32,896]{1,0:T(8,128)} %param.12) | copy-start | bytes 344068
  184.4 18.9 %copy-start.9 = (f32[4,32,896]{2,1,0:T(8,128)S(1)}, f32[4,32,896]{2,1,0:T(8,128)}, u32[]{:S(2)}) copy-start(f32[4,32,896]{2,1,0:T(8,128)} %param.11) | copy-start | bytes 1376260
  184.4 16.5 %collective-permute-start.8 = (f32[2,1,288]{1,2,0:T(8,128)S(1)}, f32[2,1,288]{1,2,0:T(8,128)S(1)}, u32[]{:S(2)}, u32[]{:S(2)}) collective-permute-start(f32[2,1,288]{1,2,0:T(8,128)S(1)} %get-tuple-element.30), channel_id=1, source_target_pairs={{0,4},{4,8},{8,12},{12,16},{16,20},{20,24},{24,28},{1,5},{5,9},{9,... | collective-permute-start | bytes 6920 | tf_op jit(solution)/shard_map/ppermute | solution.py:27
  187.9 13.1 %collective-permute-start.9 = (f32[2,1,288]{1,2,0:T(8,128)S(1)}, f32[2,1,288]{1,2,0:T(8,128)S(1)}, u32[]{:S(2)}, u32[]{:S(2)}) collective-permute-start(f32[2,1,288]{1,2,0:T(8,128)S(1)} %get-tuple-element.31), channel_id=1, source_target_pairs={{4,0},{8,4},{12,8},{16,12},{20,16},{24,20},{28,24},{5,1},{9,5},{13... | collective-permute-start | bytes 6920 | tf_op jit(solution)/shard_map/ppermute | solution.py:28
  201.3 3.3 collective-permute-start.10
  201.3 3.4 collective-permute-start.11
  314.4 5.8 %collective-permute-start.12 = (f32[5,1,896]{2,1,0:T(1,128)S(1)}, f32[5,1,896]{2,1,0:T(1,128)S(1)}, u32[]{:S(2)}, u32[]{:S(2)}) collective-permute-start(f32[5,1,896]{2,1,0:T(1,128)S(1)} %get-tuple-element.21), channel_id=1, source_target_pairs={{0,4},{4,8},{8,12},{12,16},{16,20},{20,24},{24,28},{1,5},{5,9},{9,... | collective-permute-start | bytes 53768 | tf_op jit(solution)/shard_map/ppermute | solution.py:27
  318.8 5.9 %collective-permute-start.13 = (f32[5,1,896]{2,1,0:T(1,128)S(1)}, f32[5,1,896]{2,1,0:T(1,128)S(1)}, u32[]{:S(2)}, u32[]{:S(2)}) collective-permute-start(f32[5,1,896]{2,1,0:T(1,128)S(1)} %get-tuple-element.20), channel_id=1, source_target_pairs={{4,0},{8,4},{12,8},{16,12},{20,16},{24,20},{28,24},{5,1},{9,5},{13... | collective-permute-start | bytes 53768 | tf_op jit(solution)/shard_map/ppermute | solution.py:28
  324.9 4.4 %collective-permute-start.14 = (f32[5,34,1]{2,1,0:T(8,128)S(1)}, f32[5,34,1]{2,1,0:T(8,128)S(1)}, u32[]{:S(2)}, u32[]{:S(2)}) collective-permute-start(f32[5,34,1]{2,1,0:T(8,128)S(1)} %get-tuple-element.17), channel_id=1, source_target_pairs={{0,1},{1,2},{2,3},{3,0},{4,5},{5,6},{6,7},{7,4},{8,9},{9,10},{10,1... | collective-permute-start | bytes 2048 | tf_op jit(solution)/shard_map/ppermute | solution.py:27
  325.0 4.3 %collective-permute-start.15 = (f32[5,34,1]{2,1,0:T(8,128)S(1)}, f32[5,34,1]{2,1,0:T(8,128)S(1)}, u32[]{:S(2)}, u32[]{:S(2)}) collective-permute-start(f32[5,34,1]{2,1,0:T(8,128)S(1)} %get-tuple-element.16), channel_id=1, source_target_pairs={{1,0},{2,1},{3,2},{0,3},{5,4},{6,5},{7,6},{4,7},{9,8},{10,9},{11,1... | collective-permute-start | bytes 2048 | tf_op jit(solution)/shard_map/ppermute | solution.py:28
  330.8 12.7 %copy-start.7 = (f32[768,288]{0,1:T(8,128)S(1)}, f32[768,288]{0,1:T(8,128)}, u32[]{:S(2)}) copy-start(f32[768,288]{0,1:T(8,128)} %copy-done.6) | copy-start | bytes 2654212
  330.9 6.4 %collective-permute-start.16 = (f32[5,1,896]{2,1,0:T(1,128)S(1)}, f32[5,1,896]{2,1,0:T(1,128)S(1)}, u32[]{:S(2)}, u32[]{:S(2)}) collective-permute-start(f32[5,1,896]{2,1,0:T(1,128)S(1)} %get-tuple-element.19), channel_id=1, source_target_pairs={{0,4},{4,8},{8,12},{12,16},{16,20},{20,24},{24,28},{1,5},{5,9},{9,... | collective-permute-start | bytes 53768 | tf_op jit(solution)/shard_map/ppermute | solution.py:27
  335.9 5.6 %collective-permute-start.17 = (f32[5,1,896]{2,1,0:T(1,128)S(1)}, f32[5,1,896]{2,1,0:T(1,128)S(1)}, u32[]{:S(2)}, u32[]{:S(2)}) collective-permute-start(f32[5,1,896]{2,1,0:T(1,128)S(1)} %get-tuple-element.18), channel_id=1, source_target_pairs={{4,0},{8,4},{12,8},{16,12},{20,16},{24,20},{28,24},{5,1},{9,5},{13... | collective-permute-start | bytes 53768 | tf_op jit(solution)/shard_map/ppermute | solution.py:28
  341.7 4.6 %collective-permute-start.18 = (f32[5,34,1]{2,1,0:T(8,128)S(1)}, f32[5,34,1]{2,1,0:T(8,128)S(1)}, u32[]{:S(2)}, u32[]{:S(2)}) collective-permute-start(f32[5,34,1]{2,1,0:T(8,128)S(1)} %get-tuple-element.15), channel_id=1, source_target_pairs={{0,1},{1,2},{2,3},{3,0},{4,5},{5,6},{6,7},{7,4},{8,9},{9,10},{10,1... | collective-permute-start | bytes 2048 | tf_op jit(solution)/shard_map/ppermute | solution.py:27
  341.8 4.6 %collective-permute-start.19 = (f32[5,34,1]{2,1,0:T(8,128)S(1)}, f32[5,34,1]{2,1,0:T(8,128)S(1)}, u32[]{:S(2)}, u32[]{:S(2)}) collective-permute-start(f32[5,34,1]{2,1,0:T(8,128)S(1)} %get-tuple-element.14), channel_id=1, source_target_pairs={{1,0},{2,1},{3,2},{0,3},{5,4},{6,5},{7,6},{4,7},{9,8},{10,9},{11,1... | collective-permute-start | bytes 2048 | tf_op jit(solution)/shard_map/ppermute | solution.py:28
  (3 other events, 5.4 us)
Sparse Core Ops, SparseCore 0:
  39.4 30.9 all-gather.2
  126.2 31.6 all-gather.4
where the time goes:
time: 359 us; the launch traced here: 356 us
  local copies, waits for them, and re-layouts  119 us (33%)
  waiting for transfers between devices  97.1 us (27%)
  matrix products  52.4 us (15%)
  other arithmetic  37.2 us (10%)
  starting transfers between devices  35 us (10%)
  between operations  14.8 us (4%)
    gather x2, local copies, waits for them, and re-layouts, per_device(): picked = jnp.take(bottom_rim.reshape(2, -1), flat_index, axis=1)  106 us
    dot_general x2, matrix products, per_device(): jnp.dot(lax.all_gather(lines, 'lon', axis=1, tiled=True), basis, precisio...  42.1 us
    ppermute x10, waiting for transfers between devices, padded_2(): after = lax.ppermute(first, axis, down)  39.5 us
    all_gather x2, waiting for transfers between devices, per_device(): lax.all_gather(lines, 'lon', axis=1, tiled=True)  35.3 us
    ppermute x10, starting transfers between devices, padded_2(): before = lax.ppermute(last, axis, up)  22.7 us
    ppermute x10, waiting for transfers between devices, padded_2(): before = lax.ppermute(last, axis, up)  22.2 us
    sin x1, other arithmetic, make_basis(): jnp.sin(2.0 * math.pi * sin_phase.astype(jnp.float32) / lon_total)  12.8 us
    ppermute x10, starting transfers between devices, padded_2(): after = lax.ppermute(first, axis, down)  11.9 us
  transfers between devices with their start and end apart: 22, of which 19 were waited for; matrix products, arithmetic and copies ran while one was open for 8% of the time, Pallas kernels for 0%

commit v1 on v0

v1 whole, which is shorter than its diff:
```python
import functools
import math

import jax
import jax.numpy as jnp
import ml_dtypes
import numpy as np
from jax import lax
from jax.experimental import pallas as pl
from jax.experimental.pallas import tpu as pltpu
from jax.sharding import PartitionSpec as P

STEPS = 2
OSTEPS = 2
MESH = pl.DeviceIdType.MESH
VMEM = pl.BlockSpec(memory_space=pltpu.VMEM)

advect_coef = 0.2
diffuse_coef = 0.1
flux_coef = 0.25
ocean_diffuse = 0.15
vertical_mix = 0.2


def params(cid=None):
    if cid is None:
        return pltpu.CompilerParams(vmem_limit_bytes=48 * 2**20)
    return pltpu.CompilerParams(
        collective_id=cid, has_side_effects=True, vmem_limit_bytes=48 * 2**20
    )


def split_basis(matrix):
    high = matrix.astype(ml_dtypes.bfloat16)
    low = (matrix - high.astype(np.float64)).astype(ml_dtypes.bfloat16)
    return high, low


def make_bases(lon_total):
    quarter = lon_total // 4
    n = np.arange(quarter)[:, None]

    def angle(k):
        return 2.0 * math.pi * ((n * k[None, :]) % lon_total) / lon_total

    k0 = 4 * np.arange(quarter // 2 + 1)
    k0s = 4 * np.arange(1, quarter // 2)
    m0 = np.concatenate([np.cos(angle(k0)), np.sin(angle(k0s))], axis=1)
    kk0 = np.concatenate([k0, k0s])
    s0 = np.where((kk0 == 0) | (kk0 == lon_total // 2), 1.0 / quarter, 2.0 / quarter)
    k2 = 4 * np.arange(quarter // 2) + 2
    m2 = np.concatenate([np.cos(angle(k2)), np.sin(angle(k2))], axis=1)
    kk2 = np.concatenate([k2, k2])
    s2 = np.full(quarter, 2.0 / quarter)
    k1 = 4 * np.arange(quarter) + 1
    cos1, sin1 = np.cos(angle(k1)), np.sin(angle(k1))
    m1 = np.concatenate(
        [np.concatenate([cos1, -sin1], axis=1), np.concatenate([-sin1, -cos1], axis=1)], axis=0
    )
    f1 = np.minimum(k1, lon_total - k1)
    kk1 = np.concatenate([f1, f1])
    s1 = np.full(2 * quarter, 1.0 / quarter)
    waves = np.concatenate([kk0, kk2, kk1]).astype(np.float32)
    scale = np.concatenate([s0 / 4, s2 / 4, s1 / 2]).astype(np.float32)
    return (m0, m2, m1), waves, scale


def damp_table(row_index, polar_rows, wave_numbers, lat_total, band_rows, lon_total):
    latitude_cos = jnp.sin(math.pi * (row_index.astype(jnp.float32) + 0.5) / lat_total)
    ratio = latitude_cos / math.sin(math.pi * band_rows / lat_total)
    wave_sine = jnp.sin(math.pi * wave_numbers / lon_total)
    safe_sine = jnp.where(wave_numbers > 0.5, wave_sine, 1.0)
    damping = jnp.where(
        wave_numbers[None, :] > 0.5, jnp.minimum(1.0, ratio[:, None] / safe_sine[None, :]), 1.0
    )
    listed = jnp.any(row_index[:, None] == polar_rows[None, :], axis=1)
    return jnp.where(listed[:, None], damping, 1.0)


def peer_copy(src, dst, send_sem, recv_sem, lat, lon):
    return pltpu.make_async_remote_copy(
        src_ref=src, dst_ref=dst, send_sem=send_sem, recv_sem=recv_sem,
        device_id=(lat, lon), device_id_type=MESH,
    )


def edges_kernel(lat_n, lon_n, last_row, first_row, last_col, first_col,
                 south, north, west, east, send, recv):
    lat, lon = lax.axis_index("lat"), lax.axis_index("lon")
    right, left = lax.rem(lon + 1, lon_n), lax.rem(lon + lon_n - 1, lon_n)
    has_up, has_down = lat < lat_n - 1, lat > 0
    barrier = pltpu.get_barrier_semaphore()
    for side in (left, right):
        pl.semaphore_signal(barrier, inc=1, device_id=(lat, side), device_id_type=MESH)

    @pl.when(has_up)
    def _():
        pl.semaphore_signal(barrier, inc=1, device_id=(lat + 1, lon), device_id_type=MESH)

    @pl.when(has_down)
    def _():
        pl.semaphore_signal(barrier, inc=1, device_id=(lat - 1, lon), device_id_type=MESH)

    pl.semaphore_wait(barrier, 2 + has_up.astype(jnp.int32) + has_down.astype(jnp.int32))
    go_right = peer_copy(last_col, west, send.at[0], recv.at[0], lat, right)
    go_left = peer_copy(first_col, east, send.at[1], recv.at[1], lat, left)
    go_up = peer_copy(last_row, south, send.at[2], recv.at[2], lat + 1, lon)
    go_down = peer_copy(first_row, north, send.at[3], recv.at[3], lat - 1, lon)
    go_right.start()
    go_left.start()

    @pl.when(has_up)
    def _():
        go_up.start()

    @pl.when(has_down)
    def _():
        go_down.start()

    @pl.when(has_up)
    def _():
        go_up.wait_send()
        go_down.wait_recv()

    @pl.when(jnp.logical_not(has_up))
    def _():
        north[...] = jnp.zeros_like(north)

    @pl.when(has_down)
    def _():
        go_down.wait_send()
        go_up.wait_recv()

    @pl.when(jnp.logical_not(has_down))
    def _():
        south[...] = jnp.zeros_like(south)

    go_right.wait()
    go_left.wait()


def edge_exchange(mesh_sizes, field):
    lat_n, lon_n = mesh_sizes
    levels, rows, cols = field.shape
    row_shape = jax.ShapeDtypeStruct((levels, cols), jnp.float32)
    col_shape = jax.ShapeDtypeStruct((levels, rows), jnp.float32)
    return pl.pallas_call(
        functools.partial(edges_kernel, lat_n, lon_n),
        out_shape=[row_shape, row_shape, col_shape, col_shape],
        in_specs=[VMEM] * 4,
        out_specs=[VMEM] * 4,
        scratch_shapes=[pltpu.SemaphoreType.DMA((4,)), pltpu.SemaphoreType.DMA((4,))],
        compiler_params=params(0),
        name="edges",
    )(field[:, -1], field[:, 0], field[:, :, -1], field[:, :, 0])


def atmos_step(mesh_sizes, tracer_now, wind_u, wind_v):
    south, north, west, east = edge_exchange(mesh_sizes, tracer_now)
    east_side = jnp.concatenate([tracer_now[:, :, 1:], east[:, :, None]], axis=2)
    west_side = jnp.concatenate([west[:, :, None], tracer_now[:, :, :-1]], axis=2)
    north_side = jnp.concatenate([tracer_now[:, 1:], north[:, None]], axis=1)
    south_side = jnp.concatenate([south[:, None], tracer_now[:, :-1]], axis=1)
    advect = wind_u * (east_side - west_side) + wind_v * (north_side - south_side)
    spread_sum = east_side + west_side + north_side + south_side - 4.0 * tracer_now
    return tracer_now - advect_coef * advect + diffuse_coef * spread_sum


def dot3(x, high, low, contract):
    x_high = x.astype(jnp.bfloat16)
    x_low = (x - x_high.astype(jnp.float32)).astype(jnp.bfloat16)

    def one(a, b):
        return lax.dot_general(
            a, b, (((1,), (contract,)), ((), ())), preferred_element_type=jnp.float32
        )

    return one(x_low, high) + one(x_high, low) + one(x_high, high)


def filter_kernel(lat_n, band, chunks, q, w, h0, l0, h2, l2, h1, l1, out,
                  rx, tx, send, recv, back_send, back_recv):
    lat, lon = lax.axis_index("lat"), lax.axis_index("lon")
    levels, rows, cols = q.shape
    each = levels // 4
    part = each // chunks
    polar = jnp.logical_or(lat < band, lat >= lat_n - band)

    @pl.when(jnp.logical_not(polar))
    def _():
        out[...] = q[...]

    @pl.when(polar)
    def _():
        barrier = pltpu.get_barrier_semaphore()
        for d in (1, 2, 3):
            pl.semaphore_signal(
                barrier, inc=1, device_id=(lat, lax.rem(lon + d, 4)), device_id_type=MESH
            )
        pl.semaphore_wait(barrier, 3)
        there, home = [], []
        for c in range(chunks):
            for d in (2, 3, 1):
                dest = lax.rem(lon + d, 4)
                copy = peer_copy(
                    q.at[pl.ds(dest * each + c * part, part)],
                    rx.at[lon, pl.ds(c * part, part)],
                    send.at[c, d - 1], recv.at[c, d - 1], lat, dest,
                )
                copy.start()
                there.append(copy)
        rx[pl.ds(lon, 1)] = q[pl.ds(lon * each, each)][None]
        for c in range(chunks):
            for copy in there[3 * c:3 * c + 3]:
                copy.wait_recv()
            lines = part * rows
            x = [rx[j, c * part:(c + 1) * part].reshape(lines, cols) for j in range(4)]
            even, odd = x[0] + x[2], x[1] + x[3]
            a, b = x[0] - x[2], x[1] - x[3]

            def weigh(coeffs, start):
                width = coeffs.shape[1]
                scaled = coeffs.reshape(part, rows, width) * w[:, start:start + width][None]
                return scaled.reshape(lines, width)

            f0 = weigh(dot3(even + odd, h0[...], l0[...], 0), 0)
            f2 = weigh(dot3(even - odd, h2[...], l2[...], 0), cols)
            f1 = dot3(a, h1[:cols], l1[:cols], 0) + dot3(b, h1[cols:], l1[cols:], 0)
            f1 = weigh(f1, 2 * cols)
            y0 = dot3(f0, h0[...], l0[...], 1)
            y2 = dot3(f2, h2[...], l2[...], 1)
            a = dot3(f1, h1[:cols], l1[:cols], 1)
            b = dot3(f1, h1[cols:], l1[cols:], 1)
            plus, minus = y0 + y2, y0 - y2
            for j, y in enumerate((plus + a, minus + b, plus - a, minus - b)):
                tx[j, c * part:(c + 1) * part] = y.reshape(part, rows, cols)
            for d in (2, 3, 1):
                dest = lax.rem(lon + d, 4)
                copy = peer_copy(
                    tx.at[dest, pl.ds(c * part, part)],
                    out.at[pl.ds(lon * each + c * part, part)],
                    back_send.at[c, d - 1], back_recv.at[c, d - 1], lat, dest,
                )
                copy.start()
                home.append(copy)
        out[pl.ds(lon * each, each)] = tx[pl.ds(lon, 1)][0]
        for copy in there:
            copy.wait_send()
        for d_at, copy in enumerate(home):
            copy.wait()


def polar_filter(lat_n, band, q, weights, bases):
    levels, rows, cols = q.shape
    chunks = 2
    each = levels // 4
    sems = [pltpu.SemaphoreType.DMA((chunks, 3))] * 4
    return pl.pallas_call(
        functools.partial(filter_kernel, lat_n, band, chunks),
        out_shape=jax.ShapeDtypeStruct(q.shape, jnp.float32),
        in_specs=[VMEM] * 8,
        out_specs=VMEM,
        scratch_shapes=[pltpu.VMEM((4, each, rows, cols), jnp.float32)] * 2 + sems,
        compiler_params=params(1),
        name="polar_filter",
    )(q, weights, *bases)


AROUND = [(dy, dx) for dy in (-1, 0, 1) for dx in (-1, 0, 1) if (dy, dx) != (0, 0)]


def around_exchange(lat_n, lon_n, pieces, send, recv, fill):
    lat, lon = lax.axis_index("lat"), lax.axis_index("lon")
    has = {0: None, 1: lat < lat_n - 1, -1: lat > 0}

    def guarded(dy, action):
        if dy == 0:
            action()
        else:
            pl.when(has[dy])(action)

    def side(dx):
        return lax.rem(lon + dx + lon_n, lon_n)

    barrier = pltpu.get_barrier_semaphore()

    def greet(dy):
        for dx in (-1, 0, 1):
            if (dy, dx) != (0, 0):
                pl.semaphore_signal(
                    barrier, inc=1, device_id=(lat + dy, side(dx)), device_id_type=MESH
                )

    for dy in (0, 1, -1):
        guarded(dy, functools.partial(greet, dy))
    fill(has)
    pl.semaphore_wait(barrier, 2 + 3 * (has[1].astype(jnp.int32) + has[-1].astype(jnp.int32)))
    copies = {}
    for at, (dy, dx) in enumerate(AROUND):
        src, dst = pieces(dy, dx)
        copies[dy, dx] = peer_copy(src, dst, send.at[at], recv.at[at], lat + dy, side(dx))
    for dy in (0, 1, -1):
        group = [copies[dy, dx] for dx in (-1, 0, 1) if (dy, dx) != (0, 0)]

        def begin(group=group):
            for copy in group:
                copy.start()

        guarded(dy, begin)
    for dy in (0, 1, -1):
        group = [copies[dy, dx] for dx in (-1, 0, 1) if (dy, dx) != (0, 0)]
        other = [copies[-dy, dx] for dx in (-1, 0, 1) if (dy, dx) != (0, 0)]

        def end(group=group, other=other):
            for copy in group:
                copy.wait_send()
            for copy in other:
                copy.wait_recv()

        guarded(dy, end)


def rim_kernel(lat_n, lon_n, bottom, got, send, recv):
    at = {piece: index for index, piece in enumerate(AROUND)}
    around_exchange(
        lat_n, lon_n, lambda dy, dx: (bottom, got.at[at[dy, dx]]), send, recv, lambda has: None
    )


def rim_exchange(lat_n, lon_n, bottom):
    return pl.pallas_call(
        functools.partial(rim_kernel, lat_n, lon_n),
        out_shape=jax.ShapeDtypeStruct((8,) + bottom.shape, jnp.float32),
        in_specs=[VMEM],
        out_specs=VMEM,
        scratch_shapes=[pltpu.SemaphoreType.DMA((8,)), pltpu.SemaphoreType.DMA((8,))],
        compiler_params=params(2),
        name="rim",
    )(bottom)


def remap_kernel(table, row, col, out):
    fields, table_rows, width = table.shape
    blocks = width // 128
    column_blocks = row.shape[1] // 128

    def one(step, carry):
        i = pl.multiple_of(step // column_blocks * 8, 8)
        j = pl.multiple_of(step % column_blocks * 128, 128)
        r = row[pl.ds(i, 8), pl.ds(j, 128)]
        c = col[pl.ds(i, 8), pl.ds(j, 128)]
        key = r * blocks + c // 128
        lane = c % 128
        totals = [jnp.zeros((8, 128), jnp.float32)] * fields
        for tr in range(table_rows):
            for tb in range(blocks):
                hit = key == tr * blocks + tb
                for f in range(fields):
                    line = table[f, tr:tr + 1, tb * 128:(tb + 1) * 128]
                    wide = jnp.broadcast_to(line, (8, 128))
                    got = jnp.take_along_axis(wide, lane, axis=1, mode="promise_in_bounds")
                    totals[f] = jnp.where(hit, got, totals[f])
        for f in range(fields):
            out[f, pl.ds(i, 8), pl.ds(j, 128)] = totals[f]
        return carry

    lax.fori_loop(0, row.shape[0] // 8 * column_blocks, one, 0)


def remap(table, row, col):
    return pl.pallas_call(
        remap_kernel,
        out_shape=jax.ShapeDtypeStruct((table.shape[0],) + row.shape, jnp.float32),
        in_specs=[VMEM] * 3,
        out_specs=VMEM,
        compiler_params=params(),
        name="remap",
    )(table, row, col)


def ocean_kernel(lat_n, lon_n, temp, mask, air, out, ext, send, recv):
    level_count, rows, cols = temp.shape
    high, wide = rows + 16, cols + 256

    def fill(has):
        ext[0:level_count, 8:8 + rows, 128:128 + cols] = temp[...]
        ext[level_count, 8:8 + rows, 128:128 + cols] = mask[...].astype(jnp.float32)
        ext[level_count + 1:level_count + 3, 8:8 + rows, 128:128 + cols] = air[...]

        @pl.when(jnp.logical_not(has[1]))
        def _():
            ext[:, 8 + rows:, :] = jnp.zeros((level_count + 3, 8, wide), jnp.float32)

        @pl.when(jnp.logical_not(has[-1]))
        def _():
            ext[:, :8, :] = jnp.zeros((level_count + 3, 8, wide), jnp.float32)

    source_rows = {-1: (8, 8), 0: (8, rows), 1: (rows, 8)}
    target_rows = {-1: (8 + rows, 8), 0: (8, rows), 1: (0, 8)}
    source_cols = {-1: (128, 128), 0: (128, cols), 1: (cols, 128)}
    target_cols = {-1: (128 + cols, 128), 0: (128, cols), 1: (0, 128)}

    def pieces(dy, dx):
        def view(r, c):
            return ext.at[:, pl.ds(*r), pl.ds(*c)]

        return (
            view(source_rows[dy], source_cols[dx]),
            view(target_rows[dy], target_cols[dx]),
        )

    around_exchange(lat_n, lon_n, pieces, send, recv, fill)
    sea = ext[level_count]
    air_temp = ext[level_count + 1]
    gain = sea * flux_coef * ext[level_count + 2]

    def shifts(x):
        return (
            pltpu.roll(x, wide - 1, 1), pltpu.roll(x, 1, 1),
            pltpu.roll(x, high - 1, 0), pltpu.roll(x, 1, 0),
        )

    couplings = [ocean_diffuse * sea * s for s in shifts(sea)]
    total = couplings[0] + couplings[1] + couplings[2] + couplings[3]
    mix = vertical_mix * sea
    levels = [ext[l] for l in range(level_count)]
    for _ in range(OSTEPS):
        levels[0] = levels[0] + gain * (air_temp - levels[0])
        for l in range(level_count):
            t = levels[l]
            moved = shifts(t)
            flow = couplings[0] * (moved[0] - t)
            for k in range(1, 4):
                flow = flow + couplings[k] * (moved[k] - t)
            levels[l] = t + flow
        upper = [levels[0]] + levels[:-1]
        lower = levels[1:] + [levels[-1]]
        levels = [
            t + mix * (u + d - 2.0 * t) for t, u, d in zip(levels, upper, lower)
        ]
    for l in range(level_count):
        out[l] = levels[l][8:8 + rows, 128:128 + cols]


def ocean(lat_n, lon_n, temp, mask, air):
    level_count, rows, cols = temp.shape
    return pl.pallas_call(
        functools.partial(ocean_kernel, lat_n, lon_n),
        out_shape=jax.ShapeDtypeStruct(temp.shape, jnp.float32),
        in_specs=[VMEM] * 3,
        out_specs=VMEM,
        scratch_shapes=[
            pltpu.VMEM((level_count + 3, rows + 16, cols + 256), jnp.float32),
            pltpu.SemaphoreType.DMA((8,)),
            pltpu.SemaphoreType.DMA((8,)),
        ],
        compiler_params=params(3),
        name="ocean",
    )(temp, mask, air)


def rim_table(bottom, around, lat_place, lat_n):
    got = {piece: around[index] for index, piece in enumerate(AROUND)}
    north_row = jnp.concatenate(
        [got[-1, 1][:, :1, -1:], got[-1, 0][:, :1], got[-1, -1][:, :1, :1]], axis=2
    )
    south_row = jnp.concatenate(
        [got[1, 1][:, -1:, -1:], got[1, 0][:, -1:], got[1, -1][:, -1:, :1]], axis=2
    )
    middle = jnp.concatenate([got[0, 1][:, :, -1:], bottom, got[0, -1][:, :, :1]], axis=2)
    table = jnp.concatenate([south_row, middle, north_row], axis=1)
    width = table.shape[2]
    return jnp.pad(table, ((0, 0), (0, 0), (0, -width % 128)))


def per_device(tracer, wind_u, wind_v, ocean_temp, land_mask, remap_rows, remap_cols, polar_rows):
    levels, row_count, lon_local = tracer.shape
    lat_devices = lax.axis_size("lat")
    lon_devices = lax.axis_size("lon")
    sizes = (lat_devices, lon_devices)
    lat_total = row_count * lat_devices
    lon_total = lon_local * lon_devices
    band_devices = lat_devices // 8
    band_rows = band_devices * row_count
    lat_place = lax.axis_index("lat")
    lon_place = lax.axis_index("lon")
    matrices, waves, scale = make_bases(lon_total)
    bases = []
    for matrix in matrices:
        bases.extend(jnp.asarray(part) for part in split_basis(matrix))
    own_rows = lat_place * row_count + jnp.arange(row_count, dtype=jnp.int32)
    weights = (
        damp_table(own_rows, polar_rows, jnp.asarray(waves), lat_total, band_rows, lon_total)
        * jnp.asarray(scale)[None, :]
    )
    tracer_now = tracer
    for _ in range(STEPS):
        tracer_now = atmos_step(sizes, tracer_now, wind_u, wind_v)
        tracer_now = polar_filter(lat_devices, band_devices, tracer_now, weights, bases)
    bottom = jnp.stack(
        [tracer_now[levels - 1], jnp.abs(wind_u[levels - 1]) + jnp.abs(wind_v[levels - 1]) + 0.5]
    )
    around = rim_exchange(lat_devices, lon_devices, bottom)
    table = rim_table(bottom, around, lat_place, lat_devices)
    local_row = remap_rows - lat_place * row_count + 1
    local_col = (remap_cols - lon_place * lon_local + 1) % lon_total
    air = remap(table, local_row, local_col)
    return (tracer_now, ocean(lat_devices, lon_devices, ocean_temp, land_mask, air))


def solution(mesh):
    in_specs = (
        P(None, "lat", "lon"),
        P(None, "lat", "lon"),
        P(None, "lat", "lon"),
        P(None, "lat", "lon"),
        P("lat", "lon"),
        P("lat", "lon"),
        P("lat", "lon"),
        P(),
    )
    out_specs = (P(None, "lat", "lon"), P(None, "lat", "lon"))
    return jax.shard_map(
        per_device, mesh=mesh, in_specs=in_specs, out_specs=out_specs, check_vma=False
    )
```

time: 359 us -> 120 us (0.33)
  local copies, waits for them, and re-layouts: 119 us -> 18.8 us
  waiting for transfers between devices: 97.1 us -> 0 us
  Pallas kernels: 0 us -> 96.8 us
  matrix products: 52.4 us -> 0 us
  starting transfers between devices: 35 us -> 0 us
  other arithmetic: 37.2 us -> 2.64 us
  between operations: 14.8 us -> 1.1 us
    gather x2 -> x0, local copies, waits for them, and re-layouts: 106 us -> none  [per_device(): picked = jnp.take(bottom_rim.reshape(2, -1), flat_index, axis=1)]
    pallas_call x0 -> x7, Pallas kernels: none -> 96.8 us  [the longest x2 56.2 us: polar_filter(): pl.pallas_call(functools.partial(filter_kernel, lat_n, band, chunks), out...]
    ppermute x20 -> x0, waiting for transfers between devices: 61.7 us -> none  [the longest x10 39.5 us: padded_2(): after = lax.ppermute(first, axis, down)]
    dot_general x4 -> x0, matrix products: 52.4 us -> none  [the longest x2 42.1 us: per_device(): jnp.dot(lax.all_gather(lines, 'lon', axis=1, tiled=True), basis, precisio...]
    all_gather x2 -> x0, waiting for transfers between devices: 35.3 us -> none  [per_device(): lax.all_gather(lines, 'lon', axis=1, tiled=True)]
    ppermute x20 -> x0, starting transfers between devices: 34.7 us -> none  [the longest x10 22.7 us: padded_2(): before = lax.ppermute(last, axis, up)]
    sin x1 -> x0, other arithmetic: 12.8 us -> none  [make_basis(): jnp.sin(2.0 * math.pi * sin_phase.astype(jnp.float32) / lon_total)]
    cos x1 -> x0, other arithmetic: 11 us -> none  [make_basis(): jnp.cos(2.0 * math.pi * cos_phase.astype(jnp.float32) / lon_total)]
  transfers between devices with their start and end apart: 22 -> 0, of which waited for: 19 -> 0; matrix products, arithmetic and copies ran while one was open for 8% -> 0% of each run, Pallas kernels for 0% -> 0%
where the time goes in v1:
time: 120 us; the launch traced here: 119 us
  Pallas kernels  96.8 us (81%)
  local copies, waits for them, and re-layouts  18.8 us (16%)
  other arithmetic  2.64 us (2%)
    pallas_call x2, Pallas kernels, polar_filter(): pl.pallas_call(functools.partial(filter_kernel, lat_n, band, chunks), out...  56.2 us
    pallas_call x1, Pallas kernels, ocean(): pl.pallas_call(functools.partial(ocean_kernel, lat_n, lon_n), out_shape=j...  14.2 us
    pallas_call x2, Pallas kernels, edge_exchange(): pl.pallas_call(functools.partial(edges_kernel, lat_n, lon_n), out_shape=[...  10.9 us
    unnamed x64, local copies, waits for them, and re-layouts  10.5 us
    pallas_call x1, Pallas kernels, rim_exchange(): pl.pallas_call(functools.partial(rim_kernel, lat_n, lon_n), out_shape=jax...  8.45 us
    pallas_call x1, Pallas kernels, remap(): pl.pallas_call(remap_kernel, out_shape=jax.ShapeDtypeStruct((table.shape[...  7.05 us

profile of v1, /device:TPU:0, one launch (start us, length us, event | category | flops | bytes accessed | tf_op | source)
XLA Modules:
  0.0 119.4 jit_solution(2151828290982503618)
XLA Ops:
  0.6 1.2 fusion.15
  1.8 1.3 %fusion.14 = (f32[32,24,1]{2,1,0:T(8,128)S(1)}, f32[32,24,1]{2,1,0:T(8,128)S(1)}) fusion(f32[32,24,288]{2,1,0:T(8,128)} %param.16), kind=kLoop, calls=%fused_computation.52 | loop fusion | bytes 12288 | tf_op jit(solution)/shard_map/slice | solution.py:155
  3.1 0.2 copy.68
  3.4 0.3 copy.69
  3.6 6.7 %edges.2 = (f32[32,288]{1,0:T(8,128)S(1)}, f32[32,288]{1,0:T(8,128)S(1)}, f32[32,24]{1,0:T(8,128)S(1)}, f32[32,24]{1,0:T(8,128)S(1)}) custom-call(f32[32,288]{1,0:T(8,128)S(1)} %get-tuple-element.43.last_row, f32[32,288]{1,0:T(8,128)S(1)} %get-tuple-element.42.first_row, f32[32,24]{1,0:T(8,128)S(1)} %bitcast.38, f32[32,24]{1,0:T(8,128)S(1)} %bitcast.39), custom_call_target="tpu_custom_call" | custom-call | tf_op jit(solution)/shard_map/edges/pallas_call | solution.py:147
  10.3 1.0 copy.47
  11.3 1.0 copy.49
  12.4 0.4 fusion.12
  13.1 1.0 copy-done.13
  14.1 0.4 copy-done.14
  14.5 0.4 copy-done.16
  15.1 1.0 multiply_add_fusion.1.q
  16.5 1.1 copy-done.1
  17.6 0.9 copy-done.4
  18.5 0.9 copy-done.6
  19.4 0.9 copy-done.8
  20.4 28.0 %polar_filter.2 = f32[32,24,288]{2,1,0:T(8,128)S(1)} custom-call(f32[32,24,288]{2,1,0:T(8,128)S(1)} %multiply_add_fusion.1.q, f32[24,1152]{1,0:T(8,128)S(1)} %fusion.2.w, bf16[288,288]{1,0:T(8,128)(2,1)S(1)} %copy-done.3, bf16[288,288]{1,0:T(8,128)(2,1)S(1)} %copy-done.4, bf16[288,288]{1,0:T(8,128)(2,1)S(1)} %copy-done.6, bf16[288,288]{1,0:T(8,128)(2,1)S(1)} %copy-done.8, ...), custom_call_target="tpu_custom_call" | custom-call | tf_op jit(solution)/shard_map/polar_filter/pallas_call | solution.py:258
  48.6 0.2 copy.72
  48.8 0.3 copy.73
  49.2 4.2 %edges.3 = (f32[32,288]{1,0:T(8,128)S(1)}, f32[32,288]{1,0:T(8,128)S(1)}, f32[32,24]{1,0:T(8,128)S(1)}, f32[32,24]{1,0:T(8,128)S(1)}) custom-call(f32[32,288]{1,0:T(8,128)S(1)} %bitcast.35, f32[32,288]{1,0:T(8,128)S(1)} %bitcast.34, f32[32,24]{1,0:T(8,128)S(1)} %bitcast.36, f32[32,24]{1,0:T(8,128)S(1)} %bitcast.37), custom_call_target="tpu_custom_call" | custom-call | tf_op jit(solution)/shard_map/edges/pallas_call | solution.py:147
  53.5 1.0 copy.55
  54.5 1.0 copy.57
  55.6 0.4 fusion.8
  56.2 1.0 copy-done.15
  57.2 0.4 copy-done.17
  57.8 1.1 multiply_add_fusion.q
  59.0 28.1 %polar_filter.3 = f32[32,24,288]{2,1,0:T(8,128)S(1)} custom-call(f32[32,24,288]{2,1,0:T(8,128)S(1)} %multiply_add_fusion.q, f32[24,1152]{1,0:T(8,128)S(1)} %fusion.2.w, bf16[288,288]{1,0:T(8,128)(2,1)S(1)} %copy-done.3, bf16[288,288]{1,0:T(8,128)(2,1)S(1)} %copy-done.5, bf16[288,288]{1,0:T(8,128)(2,1)S(1)} %copy-done.7, bf16[288,288]{1,0:T(8,128)(2,1)S(1)} %copy-done.9, ...), custom_call_target="tpu_custom_call" | custom-call | tf_op jit(solution)/shard_map/polar_filter/pallas_call | solution.py:258
  87.3 8.4 %rim.1 = f32[8,2,24,288]{3,2,1,0:T(8,128)S(1)} custom-call(f32[2,24,288]{2,1,0:T(8,128)S(1)} %pad_maximum_fusion.8.bottom), custom_call_target="tpu_custom_call" | custom-call | tf_op jit(solution)/shard_map/rim/pallas_call | solution.py:331
  96.3 7.0 %remap.1.air = f32[2,32,896]{2,1,0:T(8,128)S(1)} custom-call(f32[2,26,384]{2,1,0:T(8,128)S(1)} %fusion.3.table, s32[32,896]{1,0:T(8,128)S(1)} %get-tuple-element.45.row, s32[32,896]{1,0:T(8,128)S(1)} %get-tuple-element.44.col), custom_call_target="tpu_custom_call" | custom-call | tf_op jit(solution)/shard_map/remap/pallas_call | solution.py:371
  103.4 14.2 %ocean.1 = f32[4,32,896]{2,1,0:T(8,128)S(1)} custom-call(f32[4,32,896]{2,1,0:T(8,128)S(1)} %copy-done.10, s32[32,896]{1,0:T(8,128)S(1)} %copy-done.11, f32[2,32,896]{2,1,0:T(8,128)S(1)} %remap.1.air), custom_call_target="tpu_custom_call" | custom-call | tf_op jit(solution)/shard_map/ocean/pallas_call | solution.py:447
  117.6 1.0 copy.82
  118.6 0.8 copy.83
  (76 shorter events, 2.3 us)
Async XLA Ops:
  3.1 9.3 %copy-start.12 = (f32[32,24,288]{2,1,0:T(8,128)S(1)}, f32[32,24,288]{2,1,0:T(8,128)}, u32[]{:S(2)}) copy-start(f32[32,24,288]{2,1,0:T(8,128)} %param.16) | copy-start | bytes 2654212
  12.8 1.3 %copy-start.13 = (f32[32,24,288]{2,1,0:T(8,128)S(1)}, f32[32,24,288]{2,1,0:T(8,128)}, u32[]{:S(2)}) copy-start(f32[32,24,288]{2,1,0:T(8,128)} %param.16) | copy-start | bytes 2654212
  12.8 1.6 %copy-start.14 = (f32[32,24,288]{2,1,0:T(8,128)S(1)}, f32[32,24,288]{2,1,0:T(8,128)}, u32[]{:S(2)}) copy-start(f32[32,24,288]{2,1,0:T(8,128)} %param.18) | copy-start | bytes 2654212
  12.8 2.0 %copy-start.16 = (f32[32,24,288]{2,1,0:T(8,128)S(1)}, f32[32,24,288]{2,1,0:T(8,128)}, u32[]{:S(2)}) copy-start(f32[32,24,288]{2,1,0:T(8,128)} %param.17) | copy-start | bytes 2654212
  12.9 2.1 %copy-start.19 = (f32[32,24,1]{2,1,0:T(8,128)S(1)}, f32[32,24,1]{2,1,0:T(8,128)}, u32[]{:S(2)}) copy-start(f32[32,24,1]{2,1,0:T(8,128)} %copy.47) | copy-start | bytes 9220
  12.9 2.2 %copy-start.21 = (f32[32,24,1]{2,1,0:T(8,128)S(1)}, f32[32,24,1]{2,1,0:T(8,128)}, u32[]{:S(2)}) copy-start(f32[32,24,1]{2,1,0:T(8,128)} %copy.49) | copy-start | bytes 9220
  15.0 1.0 copy-start.27
  15.0 1.3 %copy-start.24 = (f32[1152]{0:T(1024)S(1)}, f32[1152]{0:T(1024)}, u32[]{:S(2)}) copy-start(f32[1152]{0:T(1024)} %constant.82.clone) | copy-start | bytes 13828
  15.0 1.3 %copy-start.25 = (f32[1152]{0:T(1024)S(1)}, f32[1152]{0:T(1024)}, u32[]{:S(2)}) copy-start(f32[1152]{0:T(1024)} %constant.89) | copy-start | bytes 13828
  15.0 1.3 %copy-start.26 = (pred[1152]{0:T(1024)(128)(4,1)S(1)}, pred[1152]{0:T(1024)(128)(4,1)}, u32[]{:S(2)}) copy-start(pred[1152]{0:T(1024)(128)(4,1)} %constant.85) | copy-start | bytes 3460
  15.0 1.4 %copy-start = (bf16[576,576]{1,0:T(8,128)(2,1)S(1)}, bf16[576,576]{1,0:T(8,128)(2,1)}, u32[]{:S(2)}) copy-start(bf16[576,576]{1,0:T(8,128)(2,1)} %constant.79.clone.h1) | copy-start | bytes 1990660
  15.0 1.4 %copy-start.3 = (bf16[288,288]{1,0:T(8,128)(2,1)S(1)}, bf16[288,288]{1,0:T(8,128)(2,1)}, u32[]{:S(2)}) copy-start(bf16[288,288]{1,0:T(8,128)(2,1)} %constant.75.clone.h0) | copy-start | bytes 497668
  16.4 1.1 copy-start.1
  17.6 0.9 copy-start.4
  18.5 0.9 copy-start.6
  19.4 0.9 copy-start.8
  55.9 1.3 %copy-start.15 = (f32[32,24,288]{2,1,0:T(8,128)S(1)}, f32[32,24,288]{2,1,0:T(8,128)}, u32[]{:S(2)}) copy-start(f32[32,24,288]{2,1,0:T(8,128)} %param.18) | copy-start | bytes 2654212
  55.9 1.6 %copy-start.17 = (f32[32,24,288]{2,1,0:T(8,128)S(1)}, f32[32,24,288]{2,1,0:T(8,128)}, u32[]{:S(2)}) copy-start(f32[32,24,288]{2,1,0:T(8,128)} %param.17) | copy-start | bytes 2654212
  56.0 1.7 %copy-start.18 = (f32[32,24,1]{2,1,0:T(8,128)S(1)}, f32[32,24,1]{2,1,0:T(8,128)}, u32[]{:S(2)}) copy-start(f32[32,24,1]{2,1,0:T(8,128)} %copy.55) | copy-start | bytes 9220
  56.0 1.8 %copy-start.20 = (f32[32,24,1]{2,1,0:T(8,128)S(1)}, f32[32,24,1]{2,1,0:T(8,128)}, u32[]{:S(2)}) copy-start(f32[32,24,1]{2,1,0:T(8,128)} %copy.57) | copy-start | bytes 9220
  57.8 1.1 copy-start.2
  57.8 1.2 copy-start.5
  57.8 1.2 %copy-start.7 = (bf16[288,288]{1,0:T(8,128)(2,1)S(1)}, bf16[288,288]{1,0:T(8,128)(2,1)}, u32[]{:S(2)}) copy-start(bf16[288,288]{1,0:T(8,128)(2,1)} %constant.77.clone.h2) | copy-start | bytes 497668
  57.8 1.3 %copy-start.9 = (bf16[288,288]{1,0:T(8,128)(2,1)S(1)}, bf16[288,288]{1,0:T(8,128)(2,1)}, u32[]{:S(2)}) copy-start(bf16[288,288]{1,0:T(8,128)(2,1)} %constant.78.clone.l2) | copy-start | bytes 497668
  87.2 9.0 %copy-start.22 = (s32[32,896]{1,0:T(8,128)S(1)}, s32[32,896]{1,0:T(8,128)}, u32[]{:S(2)}) copy-start(s32[32,896]{1,0:T(8,128)} %param.22) | copy-start | bytes 344068
  87.2 8.9 %copy-start.23 = (s32[32,896]{1,0:T(8,128)S(1)}, s32[32,896]{1,0:T(8,128)}, u32[]{:S(2)}) copy-start(s32[32,896]{1,0:T(8,128)} %param.21) | copy-start | bytes 344068
  95.7 7.6 %copy-start.10 = (f32[4,32,896]{2,1,0:T(8,128)S(1)}, f32[4,32,896]{2,1,0:T(8,128)}, u32[]{:S(2)}) copy-start(f32[4,32,896]{2,1,0:T(8,128)} %temp.1) | copy-start | bytes 1376260
  95.7 7.6 %copy-start.11 = (s32[32,896]{1,0:T(8,128)S(1)}, s32[32,896]{1,0:T(8,128)}, u32[]{:S(2)}) copy-start(s32[32,896]{1,0:T(8,128)} %mask.1) | copy-start | bytes 344068

commit v2 on v1

--- a/solution.py
+++ b/solution.py
@@ -167,6 +167,7 @@
 
 
 def dot3(x, high, low, contract):
+    lines = x.shape[0]
     x_high = x.astype(jnp.bfloat16)
     x_low = (x - x_high.astype(jnp.float32)).astype(jnp.bfloat16)
 
@@ -175,15 +176,16 @@
             a, b, (((1,), (contract,)), ((), ())), preferred_element_type=jnp.float32
         )
 
-    return one(x_low, high) + one(x_high, low) + one(x_high, high)
-
-
-def filter_kernel(lat_n, band, chunks, q, w, h0, l0, h2, l2, h1, l1, out,
-                  rx, tx, send, recv, back_send, back_recv):
+    both = one(jnp.concatenate([x_high, x_low], axis=0), high)
+    return (both[lines:] + one(x_high, low)) + both[:lines]
+
+
+def filter_kernel(lat_n, band, slots, row_of, slot_of, listed, q, w, h0, l0, h2, l2, h1, l1, out,
+                  packed, got, rx, tx, send, recv, back_send, back_recv):
     lat, lon = lax.axis_index("lat"), lax.axis_index("lon")
     levels, rows, cols = q.shape
     each = levels // 4
-    part = each // chunks
+    lines = each * slots
     polar = jnp.logical_or(lat < band, lat >= lat_n - band)
 
     @pl.when(jnp.logical_not(polar))
@@ -197,73 +199,77 @@
             pl.semaphore_signal(
                 barrier, inc=1, device_id=(lat, lax.rem(lon + d, 4)), device_id_type=MESH
             )
+        for s in range(slots):
+            packed[:, s:s + 1, :] = q[:, pl.ds(row_of[s], 1), :]
         pl.semaphore_wait(barrier, 3)
         there, home = [], []
-        for c in range(chunks):
-            for d in (2, 3, 1):
-                dest = lax.rem(lon + d, 4)
-                copy = peer_copy(
-                    q.at[pl.ds(dest * each + c * part, part)],
-                    rx.at[lon, pl.ds(c * part, part)],
-                    send.at[c, d - 1], recv.at[c, d - 1], lat, dest,
-                )
-                copy.start()
-                there.append(copy)
-        rx[pl.ds(lon, 1)] = q[pl.ds(lon * each, each)][None]
-        for c in range(chunks):
-            for copy in there[3 * c:3 * c + 3]:
-                copy.wait_recv()
-            lines = part * rows
-            x = [rx[j, c * part:(c + 1) * part].reshape(lines, cols) for j in range(4)]
-            even, odd = x[0] + x[2], x[1] + x[3]
-            a, b = x[0] - x[2], x[1] - x[3]
-
-            def weigh(coeffs, start):
-                width = coeffs.shape[1]
-                scaled = coeffs.reshape(part, rows, width) * w[:, start:start + width][None]
-                return scaled.reshape(lines, width)
-
-            f0 = weigh(dot3(even + odd, h0[...], l0[...], 0), 0)
-            f2 = weigh(dot3(even - odd, h2[...], l2[...], 0), cols)
-            f1 = dot3(a, h1[:cols], l1[:cols], 0) + dot3(b, h1[cols:], l1[cols:], 0)
-            f1 = weigh(f1, 2 * cols)
-            y0 = dot3(f0, h0[...], l0[...], 1)
-            y2 = dot3(f2, h2[...], l2[...], 1)
-            a = dot3(f1, h1[:cols], l1[:cols], 1)
-            b = dot3(f1, h1[cols:], l1[cols:], 1)
-            plus, minus = y0 + y2, y0 - y2
-            for j, y in enumerate((plus + a, minus + b, plus - a, minus - b)):
-                tx[j, c * part:(c + 1) * part] = y.reshape(part, rows, cols)
-            for d in (2, 3, 1):
-                dest = lax.rem(lon + d, 4)
-                copy = peer_copy(
-                    tx.at[dest, pl.ds(c * part, part)],
-                    out.at[pl.ds(lon * each + c * part, part)],
-                    back_send.at[c, d - 1], back_recv.at[c, d - 1], lat, dest,
-                )
-                copy.start()
-                home.append(copy)
-        out[pl.ds(lon * each, each)] = tx[pl.ds(lon, 1)][0]
+        for d in (2, 3, 1):
+            dest = lax.rem(lon + d, 4)
+            copy = peer_copy(
+                packed.at[pl.ds(dest * each, each)], rx.at[lon],
+                send.at[d - 1], recv.at[d - 1], lat, dest,
+            )
+            copy.start()
+            there.append(copy)
+        rx[pl.ds(lon, 1)] = packed[pl.ds(lon * each, each)][None]
+        for copy in there:
+            copy.wait_recv()
+        x = [rx[j].reshape(lines, cols) for j in range(4)]
+        even, odd = x[0] + x[2], x[1] + x[3]
+        a, b = x[0] - x[2], x[1] - x[3]
+
+        def weigh(coeffs, start):
+            width = coeffs.shape[1]
+            scaled = coeffs.reshape(each, slots, width) * w[:, start:start + width][None]
+            return scaled.reshape(lines, width)
+
+        f0 = weigh(dot3(even + odd, h0[...], l0[...], 0), 0)
+        f2 = weigh(dot3(even - odd, h2[...], l2[...], 0), cols)
+        f1 = dot3(a, h1[:cols], l1[:cols], 0) + dot3(b, h1[cols:], l1[cols:], 0)
+        f1 = weigh(f1, 2 * cols)
+        y0 = dot3(f0, h0[...], l0[...], 1)
+        y2 = dot3(f2, h2[...], l2[...], 1)
+        a = dot3(f1, h1[:cols], l1[:cols], 1)
+        b = dot3(f1, h1[cols:], l1[cols:], 1)
+        plus, minus = y0 + y2, y0 - y2
+        for j, y in enumerate((plus + a, minus + b, plus - a, minus - b)):
+            tx[j] = y.reshape(each, slots, cols)
+        for d in (2, 3, 1):
+            dest = lax.rem(lon + d, 4)
+            copy = peer_copy(
+                tx.at[dest], got.at[pl.ds(lon * each, each)],
+                back_send.at[d - 1], back_recv.at[d - 1], lat, dest,
+            )
+            copy.start()
+            home.append(copy)
+        got[pl.ds(lon * each, each)] = tx[pl.ds(lon, 1)][0]
         for copy in there:
             copy.wait_send()
-        for d_at, copy in enumerate(home):
+        for copy in home:
             copy.wait()
-
-
-def polar_filter(lat_n, band, q, weights, bases):
+        for r in range(rows):
+            kept = q[:, r:r + 1, :]
+            filtered = got[:, pl.ds(slot_of[r], 1), :]
+            out[:, r:r + 1, :] = jnp.where(listed[r] > 0, filtered, kept)
+
+
+def polar_filter(lat_n, band, slots, cid, q, plan, bases):
     levels, rows, cols = q.shape
-    chunks = 2
     each = levels // 4
-    sems = [pltpu.SemaphoreType.DMA((chunks, 3))] * 4
+    smem = pl.BlockSpec(memory_space=pltpu.SMEM)
+    sems = [pltpu.SemaphoreType.DMA((3,))] * 4
+    whole = pltpu.VMEM((levels, slots, cols), jnp.float32)
+    parts = pltpu.VMEM((4, each, slots, cols), jnp.float32)
+    row_of, slot_of, listed, weights = plan
     return pl.pallas_call(
-        functools.partial(filter_kernel, lat_n, band, chunks),
+        functools.partial(filter_kernel, lat_n, band, slots),
         out_shape=jax.ShapeDtypeStruct(q.shape, jnp.float32),
-        in_specs=[VMEM] * 8,
+        in_specs=[smem] * 3 + [VMEM] * 8,
         out_specs=VMEM,
-        scratch_shapes=[pltpu.VMEM((4, each, rows, cols), jnp.float32)] * 2 + sems,
-        compiler_params=params(1),
+        scratch_shapes=[whole, whole, parts, parts] + sems,
+        compiler_params=params(cid),
         name="polar_filter",
-    )(q, weights, *bases)
+    )(row_of, slot_of, listed, q, weights, *bases)
 
 
 AROUND = [(dy, dx) for dy in (-1, 0, 1) for dx in (-1, 0, 1) if (dy, dx) != (0, 0)]
@@ -322,9 +328,14 @@
 
 def rim_kernel(lat_n, lon_n, bottom, got, send, recv):
     at = {piece: index for index, piece in enumerate(AROUND)}
-    around_exchange(
-        lat_n, lon_n, lambda dy, dx: (bottom, got.at[at[dy, dx]]), send, recv, lambda has: None
-    )
+    rows = bottom.shape[1]
+    start = {-1: 0, 0: 0, 1: rows - 8}
+
+    def pieces(dy, dx):
+        span = pl.ds(start[dy], rows if dy == 0 else 8)
+        return bottom.at[:, span], got.at[at[dy, dx], :, span]
+
+    around_exchange(lat_n, lon_n, pieces, send, recv, lambda has: None)
 
 
 def rim_exchange(lat_n, lon_n, bottom):
@@ -488,15 +499,40 @@
     bases = []
     for matrix in matrices:
         bases.extend(jnp.asarray(part) for part in split_basis(matrix))
-    own_rows = lat_place * row_count + jnp.arange(row_count, dtype=jnp.int32)
-    weights = (
-        damp_table(own_rows, polar_rows, jnp.asarray(waves), lat_total, band_rows, lon_total)
-        * jnp.asarray(scale)[None, :]
-    )
-    tracer_now = tracer
-    for _ in range(STEPS):
-        tracer_now = atmos_step(sizes, tracer_now, wind_u, wind_v)
-        tracer_now = polar_filter(lat_devices, band_devices, tracer_now, weights, bases)
+    band_first = lax.broadcasted_iota(jnp.int32, (lat_devices, 1), 0) * row_count
+    inside = (polar_rows[None, :] >= band_first) & (polar_rows[None, :] < band_first + row_count)
+    most = jnp.max(jnp.sum(inside.astype(jnp.int32), axis=1))
+    local_rows = jnp.arange(row_count, dtype=jnp.int32)
+    own_rows = lat_place * row_count + local_rows
+    listed = jnp.any(own_rows[:, None] == polar_rows[None, :], axis=1)
+    before = (local_rows[None, :] < local_rows[:, None]) & listed[None, :]
+    slot_of = jnp.sum(before.astype(jnp.int32), axis=1)
+
+    def atmosphere(slots, cid, tracer_now):
+        filled = (slot_of[None, :] == jnp.arange(slots)[:, None]) & listed[None, :]
+        row_of = jnp.sum(jnp.where(filled, local_rows[None, :], 0), axis=1)
+        weights = (
+            damp_table(
+                lat_place * row_count + row_of, polar_rows, jnp.asarray(waves),
+                lat_total, band_rows, lon_total,
+            )
+            * jnp.asarray(scale)[None, :]
+        )
+        plan = (row_of, jnp.minimum(slot_of, slots - 1), listed.astype(jnp.int32), weights)
+        for _ in range(STEPS):
+            tracer_now = atmos_step(sizes, tracer_now, wind_u, wind_v)
+            tracer_now = polar_filter(
+                lat_devices, band_devices, slots, cid, tracer_now, plan, bases
+            )
+        return tracer_now
+
+    few = 16
+    tracer_now = lax.cond(
+        most <= few,
+        functools.partial(atmosphere, few, 1),
+        functools.partial(atmosphere, row_count, 4),
+        tracer,
+    )
     bottom = jnp.stack(
         [tracer_now[levels - 1], jnp.abs(wind_u[levels - 1]) + jnp.abs(wind_v[levels - 1]) + 0.5]
     )

time: 120 us -> 123 us (1.025)
  Pallas kernels: 96.8 us -> 89 us
  other arithmetic: 2.64 us -> 9.45 us
  local copies, waits for them, and re-layouts: 18.8 us -> 21.4 us
    unnamed x64 -> x10, local copies, waits for them, and re-layouts: 10.5 us -> 3.15 us
    cond x0 -> x46, local copies, waits for them, and re-layouts: none -> 7.07 us
    pallas_call x2, Pallas kernels: 56.2 us -> 50.6 us  [polar_filter(): pl.pallas_call(functools.partial(filter_kernel, lat_n, band, slots), out_...]
    another operation x0 -> x2, local copies, waits for them, and re-layouts: none -> 5.38 us
    pallas_call x1, Pallas kernels: 8.45 us -> 5.46 us  [rim_exchange(): pl.pallas_call(functools.partial(rim_kernel, lat_n, lon_n), out_shape=jax...]
    reduce_sum x0 -> x3, other arithmetic: none -> 1.73 us  [the longest x1 0.84 us: per_device(): most = jnp.max(jnp.sum(inside.astype(jnp.int32), axis=1))]
    slice x2 -> x1, local copies, waits for them, and re-layouts: 1.46 us -> 0.17 us  [edge_exchange(): field[:, :, 0]]
where the time goes in v2:
time: 123 us; the launch traced here: 122 us
  Pallas kernels  89 us (72%)
  local copies, waits for them, and re-layouts  21.4 us (17%)
  other arithmetic  9.45 us (8%)
  between operations  1.45 us (1%)
    pallas_call x2, Pallas kernels, polar_filter(): pl.pallas_call(functools.partial(filter_kernel, lat_n, band, slots), out_...  50.6 us
    pallas_call x1, Pallas kernels, ocean(): pl.pallas_call(functools.partial(ocean_kernel, lat_n, lon_n), out_shape=j...  15 us
    pallas_call x2, Pallas kernels, edge_exchange(): pl.pallas_call(functools.partial(edges_kernel, lat_n, lon_n), out_shape=[...  10.9 us
    cond x46, local copies, waits for them, and re-layouts  7.07 us
    pallas_call x1, Pallas kernels, remap(): pl.pallas_call(remap_kernel, out_shape=jax.ShapeDtypeStruct((table.shape[...  7.05 us
    pallas_call x1, Pallas kernels, rim_exchange(): pl.pallas_call(functools.partial(rim_kernel, lat_n, lon_n), out_shape=jax...  5.46 us
    another operation x2, local copies, waits for them, and re-layouts  5.38 us
    unnamed x10, local copies, waits for them, and re-layouts  3.15 us

profile of v2, /device:TPU:0, one launch (start us, length us, event | category | flops | bytes accessed | tf_op | source)
XLA Modules:
  0.0 121.9 jit_solution(9437131062041662494)
XLA Ops:
  0.6 0.8 compare_reduce_fusion.2
  1.5 0.8 convert_reduce_fusion
  2.4 0.6 reduce_max.9
  3.6 85.3 %conditional.1 = (f32[32,24,288]{2,1,0:T(8,128)}) conditional(s32[]{:T(128)} %convert_element_type.32, (s32[24,24]{1,0:T(8,128)S(1)}, pred[24]{0:T(512)(128)(4,1)S(1)}, s32[24]{0:T(128)S(1)}, f32[32,24,288]{2,1,0:T(8,128)}, f32[32,24,288]{2,1,0:T(8,128)}, /*index=5*/f32[32,24,288]{2,1,0:T(8,128)}, s32[]{:T(128)}, s32[24]{0:T(128)}) %tuple.90, ...), branch_computations={%region_3.7_spmd.clone, %region_7.11_spmd.clone} | conditional | flops 8109601 | bytes 66348272 | solution.py:530
  3.9 5.2 %copy.123 = f32[32,24,288]{1,0,2:T(8,128)} copy(f32[32,24,288]{2,1,0:T(8,128)} %get-tuple-element.152) | data formatting | bytes 1769472 | tf_op jit(solution)/shard_map
  9.1 0.7 slice_bitcast_fusion.6
  10.1 6.7 %edges.6 = (f32[32,288]{1,0:T(8,128)S(1)}, f32[32,288]{1,0:T(8,128)S(1)}, f32[32,24]{1,0:T(8,128)S(1)}, f32[32,24]{1,0:T(8,128)S(1)}) custom-call(f32[32,288]{1,0:T(8,128)S(1)} %get-tuple-element.210.last_row, f32[32,288]{1,0:T(8,128)S(1)} %get-tuple-element.209.first_row, f32[32,24]{1,0:T(8,128)S(1)} %get-tuple-element.196.last_col, ...), custom_call_target="tpu_custom_call" | custom-call | tf_op jit(solution)/shard_map/cond/branch_1_fun/edges/pallas_call | solution.py:147
  16.8 1.0 copy.126
  17.8 1.0 copy.127
  18.9 0.4 fusion.25
  19.5 1.0 copy-done.26
  21.4 1.0 multiply_add_fusion.3.q
  22.6 0.8 select_reduce_fusion.1.row_of
  23.4 0.8 compare_reduce_fusion.1
  24.3 0.7 sine_select_fusion.1
  25.0 0.7 broadcast_compare_fusion.1
  25.7 0.8 fusion.6.w
  26.6 1.1 copy-done.4
  27.7 0.9 copy-done.15
  28.6 0.9 copy-done.17
  29.5 25.3 %polar_filter.6 = f32[32,24,288]{2,1,0:T(8,128)S(1)} custom-call(s32[16]{0:T(128)S(1)} %select_reduce_fusion.1.row_of, s32[24]{0:T(128)S(1)} %broadcast_minimum_fusion.1.slot_of, s32[24]{0:T(128)S(1)} %convert_element_type.36.listed, f32[32,24,288]{2,1,0:T(8,128)S(1)} %multiply_add_fusion.3.q, f32[16,1152]{1,0:T(8,128)S(1)} %fusion.6.w, ...), custom_call_target="tpu_custom_call" | custom-call | tf_op jit(solution)/shard_map/cond/branch_1_fun/polar_filter/pallas_call | solution.py:264
  55.6 4.2 %edges.7 = (f32[32,288]{1,0:T(8,128)S(1)}, f32[32,288]{1,0:T(8,128)S(1)}, f32[32,24]{1,0:T(8,128)S(1)}, f32[32,24]{1,0:T(8,128)S(1)}) custom-call(f32[32,288]{1,0:T(8,128)S(1)} %get-tuple-element.212.last_row, f32[32,288]{1,0:T(8,128)S(1)} %get-tuple-element.211.first_row, f32[32,24]{1,0:T(8,128)S(1)} %bitcast.77, f32[32,24]{1,0:T(8,128)S(1)} %bitcast.79), custom_call_target="tpu_custom_call" | custom-call | tf_op jit(solution)/shard_map/cond/branch_1_fun/edges/pallas_call | solution.py:147
  61.0 1.1 copy-done.30
  62.5 1.1 multiply_add_fusion.2.q
  63.7 25.3 %polar_filter.7 = f32[32,24,288]{2,1,0:T(8,128)} custom-call(s32[16]{0:T(128)S(1)} %select_reduce_fusion.1.row_of, s32[24]{0:T(128)S(1)} %broadcast_minimum_fusion.1.slot_of, s32[24]{0:T(128)S(1)} %convert_element_type.36.listed, f32[32,24,288]{2,1,0:T(8,128)S(1)} %multiply_add_fusion.2.q, f32[16,1152]{1,0:T(8,128)S(1)} %copy-done.20, ...), custom_call_target="tpu_custom_call" | custom-call | tf_op jit(solution)/shard_map/cond/branch_1_fun/polar_filter/pallas_call | solution.py:264
  89.0 0.8 slice.159
  89.8 0.8 add_add_fusion
  90.6 5.5 %rim.1 = f32[8,2,24,288]{3,2,1,0:T(8,128)S(1)} custom-call(f32[2,24,288]{2,1,0:T(8,128)S(1)} %pad_maximum_fusion.16.bottom), custom_call_target="tpu_custom_call" | custom-call | tf_op jit(solution)/shard_map/rim/pallas_call | solution.py:342
  96.6 7.0 %remap.1.air = f32[2,32,896]{2,1,0:T(8,128)S(1)} custom-call(f32[2,26,384]{2,1,0:T(8,128)S(1)} %fusion.8.table, s32[32,896]{1,0:T(8,128)S(1)} %get-tuple-element.224.row, s32[32,896]{1,0:T(8,128)S(1)} %get-tuple-element.223.col), custom_call_target="tpu_custom_call" | custom-call | tf_op jit(solution)/shard_map/remap/pallas_call | solution.py:382
  103.7 15.0 %ocean.1 = f32[4,32,896]{2,1,0:T(8,128)S(1)} custom-call(f32[4,32,896]{2,1,0:T(8,128)S(1)} %copy-done.21, s32[32,896]{1,0:T(8,128)S(1)} %copy-done.22, f32[2,32,896]{2,1,0:T(8,128)S(1)} %remap.1.air), custom_call_target="tpu_custom_call" | custom-call | tf_op jit(solution)/shard_map/ocean/pallas_call | solution.py:458
  118.8 2.4 %copy.146 = f32[32,24,288]{2,1,0:T(8,128)} copy(f32[32,24,288]{2,1,0:T(8,128)} %get-tuple-element.229) | data formatting | bytes 1769472
  121.1 0.8 copy.147
  (83 shorter events, 4.6 us)
Async XLA Ops:
  3.9 5.2 %copy-start.39 = (s32[24,24]{1,0:T(8,128)}, s32[24,24]{1,0:T(8,128)S(1)}, u32[]{:S(2)}) copy-start(s32[24,24]{1,0:T(8,128)S(1)} %get-tuple-element.149) | copy-start | bytes 6916 | tf_op jit(solution)/shard_map/cond
  3.9 5.2 %copy-start.43 = (s32[24]{0:T(128)}, s32[24]{0:T(128)S(1)}, u32[]{:S(2)}) copy-start(s32[24]{0:T(128)S(1)} %get-tuple-element.151) | copy-start | bytes 292 | tf_op jit(solution)/shard_map/cond
  3.9 5.9 %copy-start.25 = (f32[32,24,288]{2,1,0:T(8,128)S(1)}, f32[32,24,288]{2,1,0:T(8,128)}, u32[]{:S(2)}) copy-start(f32[32,24,288]{2,1,0:T(8,128)} %get-tuple-element.152) | copy-start | bytes 2654212 | tf_op jit(solution)/shard_map/cond
  19.2 1.3 %copy-start.26 = (f32[32,24,288]{2,1,0:T(8,128)S(1)}, f32[32,24,288]{2,1,0:T(8,128)}, u32[]{:S(2)}) copy-start(f32[32,24,288]{2,1,0:T(8,128)} %get-tuple-element.152) | copy-start | bytes 2654212 | tf_op jit(solution)/shard_map/cond
  19.3 1.6 %copy-start.29 = (f32[32,24,288]{2,1,0:T(8,128)S(1)}, f32[32,24,288]{2,1,0:T(8,128)}, u32[]{:S(2)}) copy-start(f32[32,24,288]{2,1,0:T(8,128)} %get-tuple-element.153) | copy-start | bytes 2654212 | tf_op jit(solution)/shard_map/cond
  19.3 2.0 %copy-start.33 = (f32[32,24,288]{2,1,0:T(8,128)S(1)}, f32[32,24,288]{2,1,0:T(8,128)}, u32[]{:S(2)}) copy-start(f32[32,24,288]{2,1,0:T(8,128)} %get-tuple-element.156) | copy-start | bytes 2654212 | tf_op jit(solution)/shard_map/cond
  19.3 2.0 %copy-start.35 = (f32[32,24,1]{2,1,0:T(8,128)S(1)}, f32[32,24,1]{2,1,0:T(8,128)}, u32[]{:S(2)}) copy-start(f32[32,24,1]{2,1,0:T(8,128)} %copy.126) | copy-start | bytes 9220 | tf_op jit(solution)/shard_map/cond
  19.3 2.1 %copy-start.36 = (f32[32,24,1]{2,1,0:T(8,128)S(1)}, f32[32,24,1]{2,1,0:T(8,128)}, u32[]{:S(2)}) copy-start(f32[32,24,1]{2,1,0:T(8,128)} %copy.127) | copy-start | bytes 9220 | tf_op jit(solution)/shard_map/cond
  21.4 1.0 copy-start.40
  21.4 5.1 %copy-start.3 = (bf16[576,576]{1,0:T(8,128)(2,1)S(1)}, bf16[576,576]{1,0:T(8,128)(2,1)}, u32[]{:S(2)}) copy-start(bf16[576,576]{1,0:T(8,128)(2,1)} %constant.129.clone.4.h1) | copy-start | bytes 1990660 | tf_op jit(solution)/shard_map/cond
  21.4 5.1 %copy-start.13 = (bf16[288,288]{1,0:T(8,128)(2,1)S(1)}, bf16[288,288]{1,0:T(8,128)(2,1)}, u32[]{:S(2)}) copy-start(bf16[288,288]{1,0:T(8,128)(2,1)} %constant.125.clone.4.h0) | copy-start | bytes 497668 | tf_op jit(solution)/shard_map/cond
  21.4 5.1 %copy-start.14 = (bf16[288,288]{1,0:T(8,128)(2,1)S(1)}, bf16[288,288]{1,0:T(8,128)(2,1)}, u32[]{:S(2)}) copy-start(bf16[288,288]{1,0:T(8,128)(2,1)} %constant.126.clone.4.l0) | copy-start | bytes 497668 | tf_op jit(solution)/shard_map/cond
  26.5 28.3 %copy-start.19 = (f32[16,1152]{1,0:T(8,128)}, f32[16,1152]{1,0:T(8,128)S(1)}, u32[]{:S(2)}) copy-start(f32[16,1152]{1,0:T(8,128)S(1)} %fusion.6.w) | copy-start | bytes 221188 | tf_op jit(solution)/shard_map/cond
  26.6 1.1 copy-start.4
  27.7 0.9 copy-start.15
  28.6 0.9 copy-start.17
  60.8 1.3 %copy-start.30 = (f32[32,24,288]{2,1,0:T(8,128)S(1)}, f32[32,24,288]{2,1,0:T(8,128)}, u32[]{:S(2)}) copy-start(f32[32,24,288]{2,1,0:T(8,128)} %get-tuple-element.153) | copy-start | bytes 2654212 | tf_op jit(solution)/shard_map/cond
  60.8 1.6 %copy-start.34 = (f32[32,24,288]{2,1,0:T(8,128)S(1)}, f32[32,24,288]{2,1,0:T(8,128)}, u32[]{:S(2)}) copy-start(f32[32,24,288]{2,1,0:T(8,128)} %get-tuple-element.156) | copy-start | bytes 2654212 | tf_op jit(solution)/shard_map/cond
  62.5 1.1 copy-start.5
  62.5 1.2 copy-start.16
  62.5 1.2 %copy-start.18 = (bf16[288,288]{1,0:T(8,128)(2,1)S(1)}, bf16[288,288]{1,0:T(8,128)(2,1)}, u32[]{:S(2)}) copy-start(bf16[288,288]{1,0:T(8,128)(2,1)} %constant.128.clone.4.l2) | copy-start | bytes 497668 | tf_op jit(solution)/shard_map/cond
  62.5 1.2 %copy-start.20 = (f32[16,1152]{1,0:T(8,128)S(1)}, f32[16,1152]{1,0:T(8,128)}, u32[]{:S(2)}) copy-start(f32[16,1152]{1,0:T(8,128)} %copy-done.19) | copy-start | bytes 221188 | tf_op jit(solution)/shard_map/cond
  90.6 6.0 %copy-start.37 = (s32[32,896]{1,0:T(8,128)S(1)}, s32[32,896]{1,0:T(8,128)}, u32[]{:S(2)}) copy-start(s32[32,896]{1,0:T(8,128)} %param.24) | copy-start | bytes 344068
  90.6 6.0 %copy-start.38 = (s32[32,896]{1,0:T(8,128)S(1)}, s32[32,896]{1,0:T(8,128)}, u32[]{:S(2)}) copy-start(s32[32,896]{1,0:T(8,128)} %param.23) | copy-start | bytes 344068
  96.1 7.6 %copy-start.21 = (f32[4,32,896]{2,1,0:T(8,128)S(1)}, f32[4,32,896]{2,1,0:T(8,128)}, u32[]{:S(2)}) copy-start(f32[4,32,896]{2,1,0:T(8,128)} %temp.1) | copy-start | bytes 1376260
  96.1 7.6 %copy-start.22 = (s32[32,896]{1,0:T(8,128)S(1)}, s32[32,896]{1,0:T(8,128)}, u32[]{:S(2)}) copy-start(s32[32,896]{1,0:T(8,128)} %mask.1) | copy-start | bytes 344068

commit v3 on v2

--- a/solution.py
+++ b/solution.py
@@ -181,12 +181,32 @@
 
 
 def filter_kernel(lat_n, band, slots, row_of, slot_of, listed, q, w, h0, l0, h2, l2, h1, l1, out,
-                  packed, got, rx, tx, send, recv, back_send, back_recv):
+                  hold, go, rx, ret, back, send, recv, back_send, back_recv):
     lat, lon = lax.axis_index("lat"), lax.axis_index("lon")
     levels, rows, cols = q.shape
     each = levels // 4
     lines = each * slots
+    full, rest = cols // 128, cols % 128
+    per = 128 // rest
     polar = jnp.logical_or(lat < band, lat >= lat_n - band)
+
+    def pack(message, j):
+        base = j * each
+        for t in range(full):
+            message[j, t * each:(t + 1) * each] = hold[base:base + each, :, t * 128:(t + 1) * 128]
+        for g in range(each // per):
+            message[j, full * each + g] = jnp.concatenate(
+                [hold[base + g * per + i, :, full * 128:] for i in range(per)], axis=1
+            )
+
+    def unpack(message, j):
+        base = j * each
+        for t in range(full):
+            hold[base:base + each, :, t * 128:(t + 1) * 128] = message[j, t * each:(t + 1) * each]
+        for g in range(each // per):
+            tails = message[j, full * each + g]
+            for i in range(per):
+                hold[base + g * per + i, :, full * 128:] = tails[:, i * rest:(i + 1) * rest]
 
     @pl.when(jnp.logical_not(polar))
     def _():
@@ -200,21 +220,25 @@
                 barrier, inc=1, device_id=(lat, lax.rem(lon + d, 4)), device_id_type=MESH
             )
         for s in range(slots):
-            packed[:, s:s + 1, :] = q[:, pl.ds(row_of[s], 1), :]
+            hold[:, s:s + 1, :] = q[:, pl.ds(row_of[s], 1), :]
+        for j in range(4):
+            pack(go, j)
         pl.semaphore_wait(barrier, 3)
         there, home = [], []
         for d in (2, 3, 1):
             dest = lax.rem(lon + d, 4)
             copy = peer_copy(
-                packed.at[pl.ds(dest * each, each)], rx.at[lon],
+                go.at[dest], rx.at[lon],
                 send.at[d - 1], recv.at[d - 1], lat, dest,
             )
             copy.start()
             there.append(copy)
-        rx[pl.ds(lon, 1)] = packed[pl.ds(lon * each, each)][None]
+        rx[pl.ds(lon, 1)] = go[pl.ds(lon, 1)]
         for copy in there:
             copy.wait_recv()
-        x = [rx[j].reshape(lines, cols) for j in range(4)]
+        for j in range(4):
+            unpack(rx, j)
+        x = [hold[j * each:(j + 1) * each].reshape(lines, cols) for j in range(4)]
         even, odd = x[0] + x[2], x[1] + x[3]
         a, b = x[0] - x[2], x[1] - x[3]
 
@@ -233,23 +257,26 @@
         b = dot3(f1, h1[cols:], l1[cols:], 1)
         plus, minus = y0 + y2, y0 - y2
         for j, y in enumerate((plus + a, minus + b, plus - a, minus - b)):
-            tx[j] = y.reshape(each, slots, cols)
+            hold[j * each:(j + 1) * each] = y.reshape(each, slots, cols)
+            pack(ret, j)
         for d in (2, 3, 1):
             dest = lax.rem(lon + d, 4)
             copy = peer_copy(
-                tx.at[dest], got.at[pl.ds(lon * each, each)],
+                ret.at[dest], back.at[lon],
                 back_send.at[d - 1], back_recv.at[d - 1], lat, dest,
             )
             copy.start()
             home.append(copy)
-        got[pl.ds(lon * each, each)] = tx[pl.ds(lon, 1)][0]
+        back[pl.ds(lon, 1)] = ret[pl.ds(lon, 1)]
         for copy in there:
             copy.wait_send()
         for copy in home:
             copy.wait()
+        for j in range(4):
+            unpack(back, j)
         for r in range(rows):
             kept = q[:, r:r + 1, :]
-            filtered = got[:, pl.ds(slot_of[r], 1), :]
+            filtered = hold[:, pl.ds(slot_of[r], 1), :]
             out[:, r:r + 1, :] = jnp.where(listed[r] > 0, filtered, kept)
 
 
@@ -259,14 +286,16 @@
     smem = pl.BlockSpec(memory_space=pltpu.SMEM)
     sems = [pltpu.SemaphoreType.DMA((3,))] * 4
     whole = pltpu.VMEM((levels, slots, cols), jnp.float32)
-    parts = pltpu.VMEM((4, each, slots, cols), jnp.float32)
+    per = 128 // (cols % 128)
+    planes = cols // 128 * each + each // per
+    parts = pltpu.VMEM((4, planes, slots, 128), jnp.float32)
     row_of, slot_of, listed, weights = plan
     return pl.pallas_call(
         functools.partial(filter_kernel, lat_n, band, slots),
         out_shape=jax.ShapeDtypeStruct(q.shape, jnp.float32),
         in_specs=[smem] * 3 + [VMEM] * 8,
         out_specs=VMEM,
-        scratch_shapes=[whole, whole, parts, parts] + sems,
+        scratch_shapes=[whole] + [parts] * 4 + sems,
         compiler_params=params(cid),
         name="polar_filter",
     )(row_of, slot_of, listed, q, weights, *bases)
@@ -508,19 +537,22 @@
     before = (local_rows[None, :] < local_rows[:, None]) & listed[None, :]
     slot_of = jnp.sum(before.astype(jnp.int32), axis=1)
 
+    filled = (slot_of[None, :] == local_rows[:, None]) & listed[None, :]
+    row_of = jnp.sum(jnp.where(filled, local_rows[None, :], 0), axis=1)
+    weights = (
+        damp_table(
+            lat_place * row_count + row_of, polar_rows, jnp.asarray(waves),
+            lat_total, band_rows, lon_total,
+        )
+        * jnp.asarray(scale)[None, :]
+    )
+    listed = listed.astype(jnp.int32)
+
     def atmosphere(slots, cid, tracer_now):
-        filled = (slot_of[None, :] == jnp.arange(slots)[:, None]) & listed[None, :]
-        row_of = jnp.sum(jnp.where(filled, local_rows[None, :], 0), axis=1)
-        weights = (
-            damp_table(
-                lat_place * row_count + row_of, polar_rows, jnp.asarray(waves),
-                lat_total, band_rows, lon_total,
-            )
-            * jnp.asarray(scale)[None, :]
-        )
-        plan = (row_of, jnp.minimum(slot_of, slots - 1), listed.astype(jnp.int32), weights)
-        for _ in range(STEPS):
-            tracer_now = atmos_step(sizes, tracer_now, wind_u, wind_v)
+        plan = (row_of[:slots], jnp.minimum(slot_of, slots - 1), listed, weights[:slots])
+        for step in range(STEPS):
+            if step > 0:
+                tracer_now = atmos_step(sizes, tracer_now, wind_u, wind_v)
             tracer_now = polar_filter(
                 lat_devices, band_devices, slots, cid, tracer_now, plan, bases
             )
@@ -531,7 +563,7 @@
         most <= few,
         functools.partial(atmosphere, few, 1),
         functools.partial(atmosphere, row_count, 4),
-        tracer,
+        atmos_step(sizes, tracer, wind_u, wind_v),
     )
     bottom = jnp.stack(
         [tracer_now[levels - 1], jnp.abs(wind_u[levels - 1]) + jnp.abs(wind_v[levels - 1]) + 0.5]

time: 123 us -> 110 us (0.89)
  Pallas kernels: 89 us -> 82.1 us
  local copies, waits for them, and re-layouts: 21.4 us -> 18.5 us
  other arithmetic: 9.45 us -> 6.95 us
    pallas_call x2, Pallas kernels: 50.6 us -> 43.6 us  [polar_filter(): pl.pallas_call(functools.partial(filter_kernel, lat_n, band, slots), out_...]
    another operation x2 -> x0, local copies, waits for them, and re-layouts: 5.38 us -> none
    cond x46 -> x14, local copies, waits for them, and re-layouts: 7.07 us -> 4.18 us
    slice x1 -> x2, local copies, waits for them, and re-layouts: 0.17 us -> 2.27 us  [edge_exchange(): field[:, :, 0]]
    unnamed x10 -> x32, local copies, waits for them, and re-layouts: 3.15 us -> 5.19 us
where the time goes in v3:
time: 110 us; the launch traced here: 109 us
  Pallas kernels  82.1 us (75%)
  local copies, waits for them, and re-layouts  18.5 us (17%)
  other arithmetic  6.95 us (6%)
  between operations  1.6 us (1%)
    pallas_call x2, Pallas kernels, polar_filter(): pl.pallas_call(functools.partial(filter_kernel, lat_n, band, slots), out_...  43.6 us
    pallas_call x1, Pallas kernels, ocean(): pl.pallas_call(functools.partial(ocean_kernel, lat_n, lon_n), out_shape=j...  15 us
    pallas_call x2, Pallas kernels, edge_exchange(): pl.pallas_call(functools.partial(edges_kernel, lat_n, lon_n), out_shape=[...  10.9 us
    pallas_call x1, Pallas kernels, remap(): pl.pallas_call(remap_kernel, out_shape=jax.ShapeDtypeStruct((table.shape[...  7.05 us
    pallas_call x1, Pallas kernels, rim_exchange(): pl.pallas_call(functools.partial(rim_kernel, lat_n, lon_n), out_shape=jax...  5.46 us
    unnamed x32, local copies, waits for them, and re-layouts  5.19 us
    cond x14, local copies, waits for them, and re-layouts  4.18 us
    add x2, other arithmetic, atmos_step(): return tracer_now - advect_coef * advect + diffuse_coef * spread_sum  2.99 us

profile of v3, /device:TPU:0, one launch (start us, length us, event | category | flops | bytes accessed | tf_op | source)
XLA Modules:
  0.0 109.5 jit_solution(1241755595637900797)
XLA Ops:
  0.6 1.2 %fusion.21 = (f32[32,1,288]{2,1,0:T(1,128)S(1)}, f32[32,1,288]{2,1,0:T(1,128)S(1)}) fusion(f32[32,24,288]{2,1,0:T(8,128)} %param.18), kind=kLoop, calls=%fused_computation.77 | loop fusion | bytes 147456 | tf_op jit(solution)/shard_map/slice | solution.py:155
  1.8 1.3 %fusion.20 = (f32[32,24,1]{2,1,0:T(8,128)S(1)}, f32[32,24,1]{2,1,0:T(8,128)S(1)}) fusion(f32[32,24,288]{2,1,0:T(8,128)} %param.18), kind=kLoop, calls=%fused_computation.76 | loop fusion | bytes 12288 | tf_op jit(solution)/shard_map/slice | solution.py:155
  3.6 6.7 %edges.5 = (f32[32,288]{1,0:T(8,128)S(1)}, f32[32,288]{1,0:T(8,128)S(1)}, f32[32,24]{1,0:T(8,128)S(1)}, f32[32,24]{1,0:T(8,128)S(1)}) custom-call(f32[32,288]{1,0:T(8,128)S(1)} %get-tuple-element.144.last_row, f32[32,288]{1,0:T(8,128)S(1)} %get-tuple-element.143.first_row, f32[32,24]{1,0:T(8,128)S(1)} %bitcast.43, f32[32,24]{1,0:T(8,128)S(1)} %bitcast.46), custom_call_target="tpu_custom_call" | custom-call | tf_op jit(solution)/shard_map/edges/pallas_call | solution.py:147
  10.3 0.3 copy.78
  10.6 1.0 copy.79
  11.7 0.4 fusion.18
  12.3 1.1 copy-done.5
  13.4 0.4 copy-done.8
  13.9 2.0 %multiply_add_fusion.2 = f32[32,24,288]{2,1,0:T(8,128)} fusion(f32[32,24,288]{2,1,0:T(8,128)S(1)} %copy-done.2, f32[32,24,288]{2,1,0:T(8,128)S(1)} %copy-done.5, f32[32,23,288]{2,1,0:T(8,128)S(1)} %get-tuple-element.128, f32[32,1,288]{2,1,0:T(1,128)S(1)} %copy.81, f32[32,1,288]{2,1,0:T(1,128)S(1)} %copy.80, f32[32,23,288]{2,1,0:T(8,128)S(1)} %get-tuple-element.127, ...), kind=kLoop, calls=%fused_computation.20 | loop fusion | flops 3981312 | bytes 7077888 | tf_op jit(solution)/shard_map/add | solution.py:166
  16.6 0.8 fusion.2
  17.4 0.8 convert_reduce_fusion.1
  18.2 0.6 reduce_max.9
  19.6 57.0 %conditional.1 = (f32[32,24,288]{2,1,0:T(8,128)}) conditional(s32[]{:T(128)} %convert_element_type.22, (s32[24]{0:T(128)S(1)}, s32[24]{0:T(128)S(1)}, s32[24]{0:T(128)S(1)}, f32[32,24,288]{2,1,0:T(8,128)}, f32[24,1152]{1,0:T(8,128)S(1)}, /*index=5*/bf16[288,288]{1,0:T(8,128)(2,1)S(1)}, bf16[288,288]{1,0:T(8,128)(2,1)S(1)}, ...), branch_computations={%region_6.7_spmd, %region_7.8_spmd} | conditional | flops 3981336 | bytes 23052656 | solution.py:562
  19.8 22.2 %polar_filter.6 = f32[32,24,288]{2,1,0:T(8,128)S(1)} custom-call(s32[16]{0:T(128)S(1)} %bitcast.57, s32[24]{0:T(128)S(1)} %broadcast_minimum_fusion.1.slot_of, s32[24]{0:T(128)S(1)} %get-tuple-element.78.listed, f32[32,24,288]{2,1,0:T(8,128)} %get-tuple-element.79.q, f32[16,1152]{1,0:T(8,128)S(1)} %slice.105.w, bf16[288,288]{1,0:T(8,128)(2,1)S(1)} %get-tuple-element.81.h0, ...), custom_call_target="tpu_custom_call" | custom-call | tf_op jit(solution)/shard_map/cond/branch_1_fun/polar_filter/pallas_call | solution.py:293
  42.2 1.0 fusion.16
  43.2 1.2 %copy.96 = f32[32,24,1]{1,0,2:T(8,128)S(1)} copy(f32[32,24,1]{2,1,0:T(8,128)} %get-tuple-element.120) | data formatting | bytes 6144 | tf_op jit(solution)/shard_map/cond
  44.4 1.3 %copy.97 = f32[32,24,1]{1,0,2:T(8,128)S(1)} copy(f32[32,24,1]{2,1,0:T(8,128)} %get-tuple-element.119) | data formatting | bytes 6144 | tf_op jit(solution)/shard_map/cond
  45.6 4.2 %edges.4 = (f32[32,288]{1,0:T(8,128)S(1)}, f32[32,288]{1,0:T(8,128)S(1)}, f32[32,24]{1,0:T(8,128)S(1)}, f32[32,24]{1,0:T(8,128)S(1)}) custom-call(f32[32,288]{1,0:T(8,128)S(1)} %get-tuple-element.124.last_row, f32[32,288]{1,0:T(8,128)S(1)} %get-tuple-element.123.first_row, f32[32,24]{1,0:T(8,128)S(1)} %bitcast.45, f32[32,24]{1,0:T(8,128)S(1)} %bitcast.48), custom_call_target="tpu_custom_call" | custom-call | tf_op jit(solution)/shard_map/cond/branch_1_fun/edges/pallas_call | solution.py:147
  49.9 1.0 copy.71
  50.9 1.0 copy.73
  52.0 0.4 fusion.14
  52.6 1.1 copy-done.7
  53.6 0.4 copy-done.10
  54.2 0.9 multiply_add_fusion.1.q
  55.2 21.4 %polar_filter.7 = f32[32,24,288]{2,1,0:T(8,128)} custom-call(s32[16]{0:T(128)S(1)} %bitcast.58, s32[24]{0:T(128)S(1)} %broadcast_minimum_fusion.1.slot_of, s32[24]{0:T(128)S(1)} %get-tuple-element.78.listed, f32[32,24,288]{2,1,0:T(8,128)S(1)} %multiply_add_fusion.1.q, f32[16,1152]{1,0:T(8,128)S(1)} %slice.105.w, bf16[288,288]{1,0:T(8,128)(2,1)S(1)} %get-tuple-element.81.h0, ...), custom_call_target="tpu_custom_call" | custom-call | tf_op jit(solution)/shard_map/cond/branch_1_fun/polar_filter/pallas_call | solution.py:293
  76.6 0.8 slice.149
  77.4 0.8 add_add_fusion
  78.2 5.5 %rim.1 = f32[8,2,24,288]{3,2,1,0:T(8,128)S(1)} custom-call(f32[2,24,288]{2,1,0:T(8,128)S(1)} %pad_maximum_fusion.12.bottom), custom_call_target="tpu_custom_call" | custom-call | tf_op jit(solution)/shard_map/rim/pallas_call | solution.py:371
  84.2 7.0 %remap.1.air = f32[2,32,896]{2,1,0:T(8,128)S(1)} custom-call(f32[2,26,384]{2,1,0:T(8,128)S(1)} %fusion.3.table, s32[32,896]{1,0:T(8,128)S(1)} %get-tuple-element.146.row, s32[32,896]{1,0:T(8,128)S(1)} %get-tuple-element.145.col), custom_call_target="tpu_custom_call" | custom-call | tf_op jit(solution)/shard_map/remap/pallas_call | solution.py:411
  91.3 15.0 %ocean.1 = f32[4,32,896]{2,1,0:T(8,128)S(1)} custom-call(f32[4,32,896]{2,1,0:T(8,128)S(1)} %copy-done, s32[32,896]{1,0:T(8,128)S(1)} %copy-done.1, f32[2,32,896]{2,1,0:T(8,128)S(1)} %remap.1.air), custom_call_target="tpu_custom_call" | custom-call | tf_op jit(solution)/shard_map/ocean/pallas_call | solution.py:487
  106.4 2.4 %copy.112 = f32[32,24,288]{2,1,0:T(8,128)} copy(f32[32,24,288]{2,1,0:T(8,128)} %get-tuple-element.151) | data formatting | bytes 1769472
  108.7 0.8 copy.113
  (69 shorter events, 2.7 us)
Async XLA Ops:
  3.1 8.6 %copy-start.2 = (f32[32,24,288]{2,1,0:T(8,128)S(1)}, f32[32,24,288]{2,1,0:T(8,128)}, u32[]{:S(2)}) copy-start(f32[32,24,288]{2,1,0:T(8,128)} %param.18) | copy-start | bytes 2654212
  12.1 1.3 %copy-start.5 = (f32[32,24,288]{2,1,0:T(8,128)S(1)}, f32[32,24,288]{2,1,0:T(8,128)}, u32[]{:S(2)}) copy-start(f32[32,24,288]{2,1,0:T(8,128)} %param.20) | copy-start | bytes 2654212
  12.1 1.6 %copy-start.8 = (f32[32,24,288]{2,1,0:T(8,128)S(1)}, f32[32,24,288]{2,1,0:T(8,128)}, u32[]{:S(2)}) copy-start(f32[32,24,288]{2,1,0:T(8,128)} %param.19) | copy-start | bytes 2654212
  12.1 1.7 %copy-start.21 = (f32[32,24,1]{2,1,0:T(8,128)S(1)}, f32[32,24,1]{2,1,0:T(8,128)}, u32[]{:S(2)}) copy-start(f32[32,24,1]{2,1,0:T(8,128)} %copy.79) | copy-start | bytes 9220
  13.8 2.1 %copy-start.25 = (s32[24]{0:T(128)S(1)}, s32[24]{0:T(128)}, u32[]{:S(2)}) copy-start(s32[24]{0:T(128)} %param.25) | copy-start | bytes 292
  13.8 2.7 %copy-start.24 = (pred[1152]{0:T(1024)(128)(4,1)S(1)}, pred[1152]{0:T(1024)(128)(4,1)}, u32[]{:S(2)}) copy-start(pred[1152]{0:T(1024)(128)(4,1)} %constant.106) | copy-start | bytes 3460
  13.8 5.7 %copy-start.3 = (bf16[576,576]{1,0:T(8,128)(2,1)S(1)}, bf16[576,576]{1,0:T(8,128)(2,1)}, u32[]{:S(2)}) copy-start(bf16[576,576]{1,0:T(8,128)(2,1)} %constant.100.clone) | copy-start | bytes 1990660
  13.8 5.7 %copy-start.4 = (bf16[576,576]{1,0:T(8,128)(2,1)S(1)}, bf16[576,576]{1,0:T(8,128)(2,1)}, u32[]{:S(2)}) copy-start(bf16[576,576]{1,0:T(8,128)(2,1)} %constant.101.clone) | copy-start | bytes 1990660
  13.8 5.7 %copy-start.11 = (bf16[288,288]{1,0:T(8,128)(2,1)S(1)}, bf16[288,288]{1,0:T(8,128)(2,1)}, u32[]{:S(2)}) copy-start(bf16[288,288]{1,0:T(8,128)(2,1)} %constant.96.clone) | copy-start | bytes 497668
  13.8 5.7 %copy-start.12 = (bf16[288,288]{1,0:T(8,128)(2,1)S(1)}, bf16[288,288]{1,0:T(8,128)(2,1)}, u32[]{:S(2)}) copy-start(bf16[288,288]{1,0:T(8,128)(2,1)} %constant.97.clone) | copy-start | bytes 497668
  52.4 1.3 %copy-start.7 = (f32[32,24,288]{2,1,0:T(8,128)S(1)}, f32[32,24,288]{2,1,0:T(8,128)}, u32[]{:S(2)}) copy-start(f32[32,24,288]{2,1,0:T(8,128)} %get-tuple-element.90) | copy-start | bytes 2654212 | tf_op jit(solution)/shard_map/cond
  52.4 1.6 %copy-start.10 = (f32[32,24,288]{2,1,0:T(8,128)S(1)}, f32[32,24,288]{2,1,0:T(8,128)}, u32[]{:S(2)}) copy-start(f32[32,24,288]{2,1,0:T(8,128)} %get-tuple-element.87) | copy-start | bytes 2654212 | tf_op jit(solution)/shard_map/cond
  52.4 1.7 %copy-start.18 = (f32[32,24,1]{2,1,0:T(8,128)S(1)}, f32[32,24,1]{2,1,0:T(8,128)}, u32[]{:S(2)}) copy-start(f32[32,24,1]{2,1,0:T(8,128)} %copy.71) | copy-start | bytes 9220 | tf_op jit(solution)/shard_map/cond
  52.4 1.8 %copy-start.20 = (f32[32,24,1]{2,1,0:T(8,128)S(1)}, f32[32,24,1]{2,1,0:T(8,128)}, u32[]{:S(2)}) copy-start(f32[32,24,1]{2,1,0:T(8,128)} %copy.73) | copy-start | bytes 9220 | tf_op jit(solution)/shard_map/cond
  54.2 1.0 copy-start.14
  54.2 1.0 copy-start.16
  78.2 6.0 %copy-start.22 = (s32[32,896]{1,0:T(8,128)S(1)}, s32[32,896]{1,0:T(8,128)}, u32[]{:S(2)}) copy-start(s32[32,896]{1,0:T(8,128)} %param.24) | copy-start | bytes 344068
  78.2 6.0 %copy-start.23 = (s32[32,896]{1,0:T(8,128)S(1)}, s32[32,896]{1,0:T(8,128)}, u32[]{:S(2)}) copy-start(s32[32,896]{1,0:T(8,128)} %param.23) | copy-start | bytes 344068
  83.7 7.6 %copy-start = (f32[4,32,896]{2,1,0:T(8,128)S(1)}, f32[4,32,896]{2,1,0:T(8,128)}, u32[]{:S(2)}) copy-start(f32[4,32,896]{2,1,0:T(8,128)} %temp.1) | copy-start | bytes 1376260
  83.7 7.6 %copy-start.1 = (s32[32,896]{1,0:T(8,128)S(1)}, s32[32,896]{1,0:T(8,128)}, u32[]{:S(2)}) copy-start(s32[32,896]{1,0:T(8,128)} %mask.1) | copy-start | bytes 344068

commit v4 on v3

--- a/solution.py
+++ b/solution.py
@@ -84,8 +84,9 @@
     )
 
 
-def edges_kernel(lat_n, lon_n, last_row, first_row, last_col, first_col,
-                 south, north, west, east, send, recv):
+def stencil_kernel(lat_n, lon_n, q, wind_u, wind_v, out, last_row, first_row, last_col, first_col,
+                   south, north, west, east, send, recv):
+    levels, rows, cols = q.shape
     lat, lon = lax.axis_index("lat"), lax.axis_index("lon")
     right, left = lax.rem(lon + 1, lon_n), lax.rem(lon + lon_n - 1, lon_n)
     has_up, has_down = lat < lat_n - 1, lat > 0
@@ -101,6 +102,16 @@
     def _():
         pl.semaphore_signal(barrier, inc=1, device_id=(lat - 1, lon), device_id_type=MESH)
 
+    lane = lax.broadcasted_iota(jnp.int32, (rows, 128), 1)
+    right_tile = jnp.zeros((rows, 128), jnp.float32)
+    left_tile = jnp.zeros((rows, 128), jnp.float32)
+    for l in range(levels):
+        right_tile = jnp.where(lane == l, q[l, :, cols - 1:cols], right_tile)
+        left_tile = jnp.where(lane == l, q[l, :, 0:1], left_tile)
+        last_row[l:l + 1, :] = q[l, rows - 1:rows, :]
+        first_row[l:l + 1, :] = q[l, 0:1, :]
+    last_col[...] = right_tile
+    first_col[...] = left_tile
     pl.semaphore_wait(barrier, 2 + has_up.astype(jnp.int32) + has_down.astype(jnp.int32))
     go_right = peer_copy(last_col, west, send.at[0], recv.at[0], lat, right)
     go_left = peer_copy(first_col, east, send.at[1], recv.at[1], lat, left)
@@ -137,33 +148,32 @@
 
     go_right.wait()
     go_left.wait()
-
-
-def edge_exchange(mesh_sizes, field):
+    for l in range(levels):
+        x = q[l]
+        east_side = jnp.concatenate([x[:, 1:], east[:, l:l + 1]], axis=1)
+        west_side = jnp.concatenate([west[:, l:l + 1], x[:, :-1]], axis=1)
+        north_side = jnp.concatenate([x[1:], north[l:l + 1]], axis=0)
+        south_side = jnp.concatenate([south[l:l + 1], x[:-1]], axis=0)
+        advect = wind_u[l] * (east_side - west_side) + wind_v[l] * (north_side - south_side)
+        spread_sum = east_side + west_side + north_side + south_side - 4.0 * x
+        out[l] = x - advect_coef * advect + diffuse_coef * spread_sum
+
+
+def atmos_step(mesh_sizes, tracer_now, wind_u, wind_v):
     lat_n, lon_n = mesh_sizes
-    levels, rows, cols = field.shape
-    row_shape = jax.ShapeDtypeStruct((levels, cols), jnp.float32)
-    col_shape = jax.ShapeDtypeStruct((levels, rows), jnp.float32)
+    levels, rows, cols = tracer_now.shape
+    row_edge = pltpu.VMEM((levels, cols), jnp.float32)
+    col_edge = pltpu.VMEM((rows, 128), jnp.float32)
     return pl.pallas_call(
-        functools.partial(edges_kernel, lat_n, lon_n),
-        out_shape=[row_shape, row_shape, col_shape, col_shape],
-        in_specs=[VMEM] * 4,
-        out_specs=[VMEM] * 4,
-        scratch_shapes=[pltpu.SemaphoreType.DMA((4,)), pltpu.SemaphoreType.DMA((4,))],
+        functools.partial(stencil_kernel, lat_n, lon_n),
+        out_shape=jax.ShapeDtypeStruct(tracer_now.shape, jnp.float32),
+        in_specs=[VMEM] * 3,
+        out_specs=VMEM,
+        scratch_shapes=[row_edge, row_edge, col_edge, col_edge] * 2
+        + [pltpu.SemaphoreType.DMA((4,)), pltpu.SemaphoreType.DMA((4,))],
         compiler_params=params(0),
-        name="edges",
-    )(field[:, -1], field[:, 0], field[:, :, -1], field[:, :, 0])
-
-
-def atmos_step(mesh_sizes, tracer_now, wind_u, wind_v):
-    south, north, west, east = edge_exchange(mesh_sizes, tracer_now)
-    east_side = jnp.concatenate([tracer_now[:, :, 1:], east[:, :, None]], axis=2)
-    west_side = jnp.concatenate([west[:, :, None], tracer_now[:, :, :-1]], axis=2)
-    north_side = jnp.concatenate([tracer_now[:, 1:], north[:, None]], axis=1)
-    south_side = jnp.concatenate([south[:, None], tracer_now[:, :-1]], axis=1)
-    advect = wind_u * (east_side - west_side) + wind_v * (north_side - south_side)
-    spread_sum = east_side + west_side + north_side + south_side - 4.0 * tracer_now
-    return tracer_now - advect_coef * advect + diffuse_coef * spread_sum
+        name="stencil",
+    )(tracer_now, wind_u, wind_v)
 
 
 def dot3(x, high, low, contract):

time: 110 us -> 99.3 us (0.903)
  local copies, waits for them, and re-layouts: 18.5 us -> 5.07 us
  Pallas kernels: 82.1 us -> 86.7 us
  other arithmetic: 6.95 us -> 5.24 us
    slice x8 -> x0, local copies, waits for them, and re-layouts: 4.61 us -> none  [the longest x2 2.27 us: edge_exchange(): field[:, :, 0]]
    pallas_call x2, Pallas kernels: 10.9 us -> 15.5 us  [atmos_step(): pl.pallas_call(functools.partial(stencil_kernel, lat_n, lon_n), out_shape...]
    cond x14 -> x2, local copies, waits for them, and re-layouts: 4.18 us -> 0.01 us
    broadcast_in_dim x8 -> x0, local copies, waits for them, and re-layouts: 3.47 us -> none  [the longest x2 2.02 us: atmos_step(): west[:, :, None]]
    add x2 -> x0, other arithmetic: 2.99 us -> none  [atmos_step(): return tracer_now - advect_coef * advect + diffuse_coef * spread_sum]
    unnamed x32 -> x30, local copies, waits for them, and re-layouts: 5.19 us -> 3.12 us
where the time goes in v4:
time: 99.3 us; the launch traced here: 98.9 us
  Pallas kernels  86.7 us (87%)
  other arithmetic  5.24 us (5%)
  local copies, waits for them, and re-layouts  5.07 us (5%)
  between operations  1.58 us (2%)
    pallas_call x2, Pallas kernels, polar_filter(): pl.pallas_call(functools.partial(filter_kernel, lat_n, band, slots), out_...  43.7 us
    pallas_call x2, Pallas kernels, atmos_step(): pl.pallas_call(functools.partial(stencil_kernel, lat_n, lon_n), out_shape...  15.5 us
    pallas_call x1, Pallas kernels, ocean(): pl.pallas_call(functools.partial(ocean_kernel, lat_n, lon_n), out_shape=j...  15 us
    pallas_call x1, Pallas kernels, remap(): pl.pallas_call(remap_kernel, out_shape=jax.ShapeDtypeStruct((table.shape[...  7.05 us
    pallas_call x1, Pallas kernels, rim_exchange(): pl.pallas_call(functools.partial(rim_kernel, lat_n, lon_n), out_shape=jax...  5.46 us
    unnamed x30, local copies, waits for them, and re-layouts  3.12 us

profile of v4, /device:TPU:0, one launch (start us, length us, event | category | flops | bytes accessed | tf_op | source)
XLA Modules:
  0.0 98.9 jit_solution(10404898319027505275)
XLA Ops:
  0.6 0.8 compare_reduce_fusion.1
  1.5 0.1 convert_reduce_fusion
  1.6 0.1 select_reduce_fusion
  1.7 0.1 sine_multiply_fusion
  1.8 0.8 compare_reduce_fusion
  2.6 1.5 %fusion.2 = f32[24,1152]{1,0:T(8,128)} fusion(f32[1152]{0:T(1024)} %constant.92, f32[1152]{0:T(1024)} %constant.85.clone, f32[24]{0:T(128)S(1)} %get-tuple-element.87, pred[24]{0:T(512)(128)(4,1)S(1)} %compare_reduce_fusion, pred[1152]{0:T(1024)(128)(4,1)} %constant.88), kind=kLoop, calls=%fused_computation.8 | loop fusion | flops 138240 | bytes 121080 | tf_op jit(solution)/shard_map/mul | solution.py:553
  4.1 1.3 %copy-done = f32[32,24,288]{2,1,0:T(8,128)S(1)} copy-done((f32[32,24,288]{2,1,0:T(8,128)S(1)}, f32[32,24,288]{2,1,0:T(8,128)}, u32[]{:S(2)}) %copy-start) | copy-done | bytes 884760
  5.4 0.0 copy-start.9
  5.4 0.0 copy-start.10
  5.4 0.0 copy-start.11
  5.4 0.0 copy-start.12
  5.4 10.3 %stencil.5 = f32[32,24,288]{2,1,0:T(8,128)} custom-call(f32[32,24,288]{2,1,0:T(8,128)S(1)} %copy-done, f32[32,24,288]{2,1,0:T(8,128)} %wind_u.1, f32[32,24,288]{2,1,0:T(8,128)} %wind_v.1), custom_call_target="tpu_custom_call" | custom-call | tf_op jit(solution)/shard_map/stencil/pallas_call | solution.py:167
  15.8 0.2 convert_reduce_fusion.1
  16.0 0.6 reduce_max.9
  17.3 50.0 %conditional.1 = (f32[32,24,288]{2,1,0:T(8,128)}) conditional(s32[]{:T(128)} %convert_element_type.22, (s32[24]{0:T(128)S(1)}, s32[24]{0:T(128)S(1)}, s32[24]{0:T(128)S(1)}, f32[32,24,288]{2,1,0:T(8,128)}, f32[24,1152]{1,0:T(8,128)}, /*index=5*/bf16[288,288]{1,0:T(8,128)(2,1)S(1)}, bf16[288,288]{1,0:T(8,128)(2,1)S(1)}, ...), branch_computations={%region_6.7_spmd, %region_7.8_spmd} | conditional | flops 24 | bytes 3981568 | solution.py:572
  17.3 0.9 slice.49.w
  18.2 22.4 %polar_filter.6.q = f32[32,24,288]{2,1,0:T(8,128)S(1)} custom-call(s32[16]{0:T(128)S(1)} %bitcast.17, s32[24]{0:T(128)S(1)} %broadcast_minimum_fusion.1.slot_of, s32[24]{0:T(128)S(1)} %get-tuple-element.74.listed, f32[32,24,288]{2,1,0:T(8,128)} %get-tuple-element.75.q, f32[16,1152]{1,0:T(8,128)S(1)} %slice.49.w, bf16[288,288]{1,0:T(8,128)(2,1)S(1)} %get-tuple-element.77.h0, ...), custom_call_target="tpu_custom_call" | custom-call | tf_op jit(solution)/shard_map/cond/branch_1_fun/polar_filter/pallas_call | solution.py:303
  40.6 5.1 %stencil.4.q = f32[32,24,288]{2,1,0:T(8,128)S(1)} custom-call(f32[32,24,288]{2,1,0:T(8,128)S(1)} %polar_filter.6.q, f32[32,24,288]{2,1,0:T(8,128)S(1)} %get-tuple-element.83.wind_u, f32[32,24,288]{2,1,0:T(8,128)S(1)} %copy-done.7), custom_call_target="tpu_custom_call" | custom-call | tf_op jit(solution)/shard_map/cond/branch_1_fun/stencil/pallas_call | solution.py:167
  45.8 21.4 %polar_filter.7 = f32[32,24,288]{2,1,0:T(8,128)} custom-call(s32[16]{0:T(128)S(1)} %bitcast.18, s32[24]{0:T(128)S(1)} %broadcast_minimum_fusion.1.slot_of, s32[24]{0:T(128)S(1)} %get-tuple-element.74.listed, f32[32,24,288]{2,1,0:T(8,128)S(1)} %stencil.4.q, f32[16,1152]{1,0:T(8,128)S(1)} %slice.49.w, bf16[288,288]{1,0:T(8,128)(2,1)S(1)} %get-tuple-element.77.h0, ...), custom_call_target="tpu_custom_call" | custom-call | tf_op jit(solution)/shard_map/cond/branch_1_fun/polar_filter/pallas_call | solution.py:303
  67.4 0.8 slice.69
  68.1 0.8 add_add_fusion
  68.9 0.0 copy-start.15
  68.9 5.5 %rim.1 = f32[8,2,24,288]{3,2,1,0:T(8,128)S(1)} custom-call(f32[2,24,288]{2,1,0:T(8,128)S(1)} %pad_maximum_fusion.bottom), custom_call_target="tpu_custom_call" | custom-call | tf_op jit(solution)/shard_map/rim/pallas_call | solution.py:381
  74.5 0.1 slice.91
  74.6 0.1 slice.88
  74.7 0.1 slice.93
  74.7 0.1 fusion.3.table
  74.9 0.1 add_select_fusion
  75.0 7.0 %remap.1.air = f32[2,32,896]{2,1,0:T(8,128)S(1)} custom-call(f32[2,26,384]{2,1,0:T(8,128)S(1)} %fusion.3.table, s32[32,896]{1,0:T(8,128)S(1)} %get-tuple-element.100.row, s32[32,896]{1,0:T(8,128)S(1)} %get-tuple-element.99.col), custom_call_target="tpu_custom_call" | custom-call | tf_op jit(solution)/shard_map/remap/pallas_call | solution.py:421
  82.1 15.0 %ocean.1 = f32[4,32,896]{2,1,0:T(8,128)S(1)} custom-call(f32[4,32,896]{2,1,0:T(8,128)S(1)} %copy-done.1, s32[32,896]{1,0:T(8,128)S(1)} %copy-done.2, f32[2,32,896]{2,1,0:T(8,128)S(1)} %remap.1.air), custom_call_target="tpu_custom_call" | custom-call | tf_op jit(solution)/shard_map/ocean/pallas_call | solution.py:497
  97.1 1.0 %copy.22 = f32[32,24,288]{2,1,0:T(8,128)} copy(f32[32,24,288]{2,1,0:T(8,128)S(1)} %copy-done.8) | data formatting | bytes 1769472
  98.1 0.8 copy.23
  (35 shorter events, 0.1 us)
Async XLA Ops:
  4.1 1.3 %copy-start = (f32[32,24,288]{2,1,0:T(8,128)S(1)}, f32[32,24,288]{2,1,0:T(8,128)}, u32[]{:S(2)}) copy-start(f32[32,24,288]{2,1,0:T(8,128)} %q.1) | copy-start | bytes 2654212
  5.4 10.4 %copy-start.16 = (s32[24]{0:T(128)S(1)}, s32[24]{0:T(128)}, u32[]{:S(2)}) copy-start(s32[24]{0:T(128)} %param.25) | copy-start | bytes 292
  5.4 11.9 %copy-start.3 = (bf16[576,576]{1,0:T(8,128)(2,1)S(1)}, bf16[576,576]{1,0:T(8,128)(2,1)}, u32[]{:S(2)}) copy-start(bf16[576,576]{1,0:T(8,128)(2,1)} %constant.82.clone) | copy-start | bytes 1990660
  5.4 11.9 %copy-start.4 = (bf16[576,576]{1,0:T(8,128)(2,1)S(1)}, bf16[576,576]{1,0:T(8,128)(2,1)}, u32[]{:S(2)}) copy-start(bf16[576,576]{1,0:T(8,128)(2,1)} %constant.83.clone) | copy-start | bytes 1990660
  5.4 11.9 %copy-start.5 = (f32[32,24,288]{2,1,0:T(8,128)S(1)}, f32[32,24,288]{2,1,0:T(8,128)}, u32[]{:S(2)}) copy-start(f32[32,24,288]{2,1,0:T(8,128)} %wind_u.1) | copy-start | bytes 2654212
  5.4 11.9 %copy-start.9 = (bf16[288,288]{1,0:T(8,128)(2,1)S(1)}, bf16[288,288]{1,0:T(8,128)(2,1)}, u32[]{:S(2)}) copy-start(bf16[288,288]{1,0:T(8,128)(2,1)} %constant.78.clone) | copy-start | bytes 497668
  5.4 11.9 %copy-start.10 = (bf16[288,288]{1,0:T(8,128)(2,1)S(1)}, bf16[288,288]{1,0:T(8,128)(2,1)}, u32[]{:S(2)}) copy-start(bf16[288,288]{1,0:T(8,128)(2,1)} %constant.79.clone) | copy-start | bytes 497668
  5.4 11.9 %copy-start.11 = (bf16[288,288]{1,0:T(8,128)(2,1)S(1)}, bf16[288,288]{1,0:T(8,128)(2,1)}, u32[]{:S(2)}) copy-start(bf16[288,288]{1,0:T(8,128)(2,1)} %constant.80.clone) | copy-start | bytes 497668
  5.4 11.9 %copy-start.12 = (bf16[288,288]{1,0:T(8,128)(2,1)S(1)}, bf16[288,288]{1,0:T(8,128)(2,1)}, u32[]{:S(2)}) copy-start(bf16[288,288]{1,0:T(8,128)(2,1)} %constant.81.clone) | copy-start | bytes 497668
  18.2 22.4 %copy-start.7 = (f32[32,24,288]{2,1,0:T(8,128)S(1)}, f32[32,24,288]{2,1,0:T(8,128)}, u32[]{:S(2)}) copy-start(f32[32,24,288]{2,1,0:T(8,128)} %get-tuple-element.84.wind_v) | copy-start | bytes 2654212 | tf_op jit(solution)/shard_map/cond
  68.9 6.0 %copy-start.14 = (s32[32,896]{1,0:T(8,128)S(1)}, s32[32,896]{1,0:T(8,128)}, u32[]{:S(2)}) copy-start(s32[32,896]{1,0:T(8,128)} %param.24) | copy-start | bytes 344068
  68.9 6.0 %copy-start.15 = (s32[32,896]{1,0:T(8,128)S(1)}, s32[32,896]{1,0:T(8,128)}, u32[]{:S(2)}) copy-start(s32[32,896]{1,0:T(8,128)} %param.23) | copy-start | bytes 344068
  74.4 7.6 %copy-start.1 = (f32[4,32,896]{2,1,0:T(8,128)S(1)}, f32[4,32,896]{2,1,0:T(8,128)}, u32[]{:S(2)}) copy-start(f32[4,32,896]{2,1,0:T(8,128)} %temp.1) | copy-start | bytes 1376260
  74.4 7.6 %copy-start.2 = (s32[32,896]{1,0:T(8,128)S(1)}, s32[32,896]{1,0:T(8,128)}, u32[]{:S(2)}) copy-start(s32[32,896]{1,0:T(8,128)} %mask.1) | copy-start | bytes 344068
  74.9 22.2 %copy-start.8 = (f32[32,24,288]{2,1,0:T(8,128)S(1)}, f32[32,24,288]{2,1,0:T(8,128)}, u32[]{:S(2)}) copy-start(f32[32,24,288]{2,1,0:T(8,128)} %get-tuple-element.105) | copy-start | bytes 2654212

commit v5 on v4

--- a/solution.py
+++ b/solution.py
@@ -460,36 +460,46 @@
         )
 
     around_exchange(lat_n, lon_n, pieces, send, recv, fill)
-    sea = ext[level_count]
-    air_temp = ext[level_count + 1]
-    gain = sea * flux_coef * ext[level_count + 2]
+    lane = lax.broadcasted_iota(jnp.int32, (high, 128), 1)
+    sub = lax.broadcasted_iota(jnp.int32, (8, cols + 128), 0)
+
+    def ring(f):
+        sides = jnp.where(lane < 64, ext[f, :, 128 + cols:], ext[f, :, :128])
+        x = jnp.concatenate([ext[f, :, 128:128 + cols], sides], axis=1)
+        ends = jnp.where(sub < 4, x[8 + rows:], x[:8])
+        return jnp.concatenate([x[8:8 + rows], ends], axis=0)
+
+    sea = ring(level_count)
+    air_temp = ring(level_count + 1)
+    gain = sea * flux_coef * ring(level_count + 2)
+    ring_high, ring_wide = rows + 8, cols + 128
 
     def shifts(x):
         return (
-            pltpu.roll(x, wide - 1, 1), pltpu.roll(x, 1, 1),
-            pltpu.roll(x, high - 1, 0), pltpu.roll(x, 1, 0),
+            pltpu.roll(x, ring_wide - 1, 1), pltpu.roll(x, 1, 1),
+            pltpu.roll(x, ring_high - 1, 0), pltpu.roll(x, 1, 0),
         )
 
     couplings = [ocean_diffuse * sea * s for s in shifts(sea)]
-    total = couplings[0] + couplings[1] + couplings[2] + couplings[3]
+    keep = 1.0 - (couplings[0] + couplings[1] + couplings[2] + couplings[3])
     mix = vertical_mix * sea
-    levels = [ext[l] for l in range(level_count)]
+    levels = [ring(l) for l in range(level_count)]
     for _ in range(OSTEPS):
         levels[0] = levels[0] + gain * (air_temp - levels[0])
         for l in range(level_count):
             t = levels[l]
             moved = shifts(t)
-            flow = couplings[0] * (moved[0] - t)
-            for k in range(1, 4):
-                flow = flow + couplings[k] * (moved[k] - t)
-            levels[l] = t + flow
+            spread = keep * t
+            for k in range(4):
+                spread = spread + couplings[k] * moved[k]
+            levels[l] = spread
         upper = [levels[0]] + levels[:-1]
         lower = levels[1:] + [levels[-1]]
         levels = [
             t + mix * (u + d - 2.0 * t) for t, u, d in zip(levels, upper, lower)
         ]
     for l in range(level_count):
-        out[l] = levels[l][8:8 + rows, 128:128 + cols]
+        out[l] = levels[l][:rows, :cols]
 
 
 def ocean(lat_n, lon_n, temp, mask, air):

time: 99.3 us -> 99 us (level)
  no operation moved by 1% of the time
where the time goes in v5:
time: 99 us; the launch traced here: 98.6 us
  Pallas kernels  86.5 us (87%)
  other arithmetic  5.24 us (5%)
  local copies, waits for them, and re-layouts  5.07 us (5%)
  between operations  1.58 us (2%)
    pallas_call x2, Pallas kernels, polar_filter(): pl.pallas_call(functools.partial(filter_kernel, lat_n, band, slots), out_...  43.7 us
    pallas_call x2, Pallas kernels, atmos_step(): pl.pallas_call(functools.partial(stencil_kernel, lat_n, lon_n), out_shape...  15.5 us
    pallas_call x1, Pallas kernels, ocean(): pl.pallas_call(functools.partial(ocean_kernel, lat_n, lon_n), out_shape=j...  14.7 us
    pallas_call x1, Pallas kernels, remap(): pl.pallas_call(remap_kernel, out_shape=jax.ShapeDtypeStruct((table.shape[...  7.05 us
    pallas_call x1, Pallas kernels, rim_exchange(): pl.pallas_call(functools.partial(rim_kernel, lat_n, lon_n), out_shape=jax...  5.46 us
    unnamed x30, local copies, waits for them, and re-layouts  3.12 us

profile of v5, /device:TPU:0, one launch (start us, length us, event | category | flops | bytes accessed | tf_op | source)
XLA Modules:
  0.0 98.6 jit_solution(12762834620505031416)
XLA Ops:
  0.6 0.8 compare_reduce_fusion.1
  1.5 0.1 convert_reduce_fusion
  1.6 0.1 select_reduce_fusion
  1.7 0.1 sine_multiply_fusion
  1.8 0.8 compare_reduce_fusion
  2.6 1.5 %fusion.2 = f32[24,1152]{1,0:T(8,128)} fusion(f32[1152]{0:T(1024)} %constant.92, f32[1152]{0:T(1024)} %constant.85.clone, f32[24]{0:T(128)S(1)} %get-tuple-element.87, pred[24]{0:T(512)(128)(4,1)S(1)} %compare_reduce_fusion, pred[1152]{0:T(1024)(128)(4,1)} %constant.88), kind=kLoop, calls=%fused_computation.8 | loop fusion | flops 138240 | bytes 121080 | tf_op jit(solution)/shard_map/mul | solution.py:563
  4.1 1.3 %copy-done = f32[32,24,288]{2,1,0:T(8,128)S(1)} copy-done((f32[32,24,288]{2,1,0:T(8,128)S(1)}, f32[32,24,288]{2,1,0:T(8,128)}, u32[]{:S(2)}) %copy-start) | copy-done | bytes 884760
  5.4 0.0 copy-start.9
  5.4 0.0 copy-start.10
  5.4 0.0 copy-start.11
  5.4 0.0 copy-start.12
  5.4 10.3 %stencil.5 = f32[32,24,288]{2,1,0:T(8,128)} custom-call(f32[32,24,288]{2,1,0:T(8,128)S(1)} %copy-done, f32[32,24,288]{2,1,0:T(8,128)} %wind_u.1, f32[32,24,288]{2,1,0:T(8,128)} %wind_v.1), custom_call_target="tpu_custom_call" | custom-call | tf_op jit(solution)/shard_map/stencil/pallas_call | solution.py:167
  15.8 0.2 convert_reduce_fusion.1
  16.0 0.6 reduce_max.9
  17.3 50.0 %conditional.1 = (f32[32,24,288]{2,1,0:T(8,128)}) conditional(s32[]{:T(128)} %convert_element_type.22, (s32[24]{0:T(128)S(1)}, s32[24]{0:T(128)S(1)}, s32[24]{0:T(128)S(1)}, f32[32,24,288]{2,1,0:T(8,128)}, f32[24,1152]{1,0:T(8,128)}, /*index=5*/bf16[288,288]{1,0:T(8,128)(2,1)S(1)}, bf16[288,288]{1,0:T(8,128)(2,1)S(1)}, ...), branch_computations={%region_6.7_spmd, %region_7.8_spmd} | conditional | flops 24 | bytes 3981568 | solution.py:582
  17.3 0.9 slice.49.w
  18.2 22.4 %polar_filter.6.q = f32[32,24,288]{2,1,0:T(8,128)S(1)} custom-call(s32[16]{0:T(128)S(1)} %bitcast.17, s32[24]{0:T(128)S(1)} %broadcast_minimum_fusion.1.slot_of, s32[24]{0:T(128)S(1)} %get-tuple-element.74.listed, f32[32,24,288]{2,1,0:T(8,128)} %get-tuple-element.75.q, f32[16,1152]{1,0:T(8,128)S(1)} %slice.49.w, bf16[288,288]{1,0:T(8,128)(2,1)S(1)} %get-tuple-element.77.h0, ...), custom_call_target="tpu_custom_call" | custom-call | tf_op jit(solution)/shard_map/cond/branch_1_fun/polar_filter/pallas_call | solution.py:303
  40.6 5.1 %stencil.4.q = f32[32,24,288]{2,1,0:T(8,128)S(1)} custom-call(f32[32,24,288]{2,1,0:T(8,128)S(1)} %polar_filter.6.q, f32[32,24,288]{2,1,0:T(8,128)S(1)} %get-tuple-element.83.wind_u, f32[32,24,288]{2,1,0:T(8,128)S(1)} %copy-done.7), custom_call_target="tpu_custom_call" | custom-call | tf_op jit(solution)/shard_map/cond/branch_1_fun/stencil/pallas_call | solution.py:167
  45.8 21.4 %polar_filter.7 = f32[32,24,288]{2,1,0:T(8,128)} custom-call(s32[16]{0:T(128)S(1)} %bitcast.18, s32[24]{0:T(128)S(1)} %broadcast_minimum_fusion.1.slot_of, s32[24]{0:T(128)S(1)} %get-tuple-element.74.listed, f32[32,24,288]{2,1,0:T(8,128)S(1)} %stencil.4.q, f32[16,1152]{1,0:T(8,128)S(1)} %slice.49.w, bf16[288,288]{1,0:T(8,128)(2,1)S(1)} %get-tuple-element.77.h0, ...), custom_call_target="tpu_custom_call" | custom-call | tf_op jit(solution)/shard_map/cond/branch_1_fun/polar_filter/pallas_call | solution.py:303
  67.4 0.8 slice.69
  68.1 0.8 add_add_fusion
  68.9 0.0 copy-start.14
  69.0 5.5 %rim.1 = f32[8,2,24,288]{3,2,1,0:T(8,128)S(1)} custom-call(f32[2,24,288]{2,1,0:T(8,128)S(1)} %pad_maximum_fusion.bottom), custom_call_target="tpu_custom_call" | custom-call | tf_op jit(solution)/shard_map/rim/pallas_call | solution.py:381
  74.5 0.1 slice.91
  74.6 0.1 slice.88
  74.7 0.1 slice.93
  74.8 0.1 fusion.3.table
  74.9 0.1 add_select_fusion
  75.0 7.0 %remap.1.air = f32[2,32,896]{2,1,0:T(8,128)S(1)} custom-call(f32[2,26,384]{2,1,0:T(8,128)S(1)} %fusion.3.table, s32[32,896]{1,0:T(8,128)S(1)} %get-tuple-element.100.row, s32[32,896]{1,0:T(8,128)S(1)} %get-tuple-element.99.col), custom_call_target="tpu_custom_call" | custom-call | tf_op jit(solution)/shard_map/remap/pallas_call | solution.py:421
  82.1 14.7 %ocean.1 = f32[4,32,896]{2,1,0:T(8,128)S(1)} custom-call(f32[4,32,896]{2,1,0:T(8,128)S(1)} %copy-done.1, s32[32,896]{1,0:T(8,128)S(1)} %copy-done.2, f32[2,32,896]{2,1,0:T(8,128)S(1)} %remap.1.air), custom_call_target="tpu_custom_call" | custom-call | tf_op jit(solution)/shard_map/ocean/pallas_call | solution.py:507
  96.8 1.0 %copy.22 = f32[32,24,288]{2,1,0:T(8,128)} copy(f32[32,24,288]{2,1,0:T(8,128)S(1)} %copy-done.8) | data formatting | bytes 1769472
  97.8 0.8 copy.23
  (35 shorter events, 0.1 us)
Async XLA Ops:
  4.1 1.3 %copy-start = (f32[32,24,288]{2,1,0:T(8,128)S(1)}, f32[32,24,288]{2,1,0:T(8,128)}, u32[]{:S(2)}) copy-start(f32[32,24,288]{2,1,0:T(8,128)} %q.1) | copy-start | bytes 2654212
  5.4 10.4 %copy-start.16 = (s32[24]{0:T(128)S(1)}, s32[24]{0:T(128)}, u32[]{:S(2)}) copy-start(s32[24]{0:T(128)} %param.25) | copy-start | bytes 292
  5.4 11.9 %copy-start.3 = (bf16[576,576]{1,0:T(8,128)(2,1)S(1)}, bf16[576,576]{1,0:T(8,128)(2,1)}, u32[]{:S(2)}) copy-start(bf16[576,576]{1,0:T(8,128)(2,1)} %constant.82.clone) | copy-start | bytes 1990660
  5.4 11.9 %copy-start.4 = (bf16[576,576]{1,0:T(8,128)(2,1)S(1)}, bf16[576,576]{1,0:T(8,128)(2,1)}, u32[]{:S(2)}) copy-start(bf16[576,576]{1,0:T(8,128)(2,1)} %constant.83.clone) | copy-start | bytes 1990660
  5.4 11.9 %copy-start.5 = (f32[32,24,288]{2,1,0:T(8,128)S(1)}, f32[32,24,288]{2,1,0:T(8,128)}, u32[]{:S(2)}) copy-start(f32[32,24,288]{2,1,0:T(8,128)} %wind_u.1) | copy-start | bytes 2654212
  5.4 11.9 %copy-start.9 = (bf16[288,288]{1,0:T(8,128)(2,1)S(1)}, bf16[288,288]{1,0:T(8,128)(2,1)}, u32[]{:S(2)}) copy-start(bf16[288,288]{1,0:T(8,128)(2,1)} %constant.78.clone) | copy-start | bytes 497668
  5.4 11.9 %copy-start.10 = (bf16[288,288]{1,0:T(8,128)(2,1)S(1)}, bf16[288,288]{1,0:T(8,128)(2,1)}, u32[]{:S(2)}) copy-start(bf16[288,288]{1,0:T(8,128)(2,1)} %constant.79.clone) | copy-start | bytes 497668
  5.4 11.9 %copy-start.11 = (bf16[288,288]{1,0:T(8,128)(2,1)S(1)}, bf16[288,288]{1,0:T(8,128)(2,1)}, u32[]{:S(2)}) copy-start(bf16[288,288]{1,0:T(8,128)(2,1)} %constant.80.clone) | copy-start | bytes 497668
  5.4 11.9 %copy-start.12 = (bf16[288,288]{1,0:T(8,128)(2,1)S(1)}, bf16[288,288]{1,0:T(8,128)(2,1)}, u32[]{:S(2)}) copy-start(bf16[288,288]{1,0:T(8,128)(2,1)} %constant.81.clone) | copy-start | bytes 497668
  18.2 22.4 %copy-start.7 = (f32[32,24,288]{2,1,0:T(8,128)S(1)}, f32[32,24,288]{2,1,0:T(8,128)}, u32[]{:S(2)}) copy-start(f32[32,24,288]{2,1,0:T(8,128)} %get-tuple-element.84.wind_v) | copy-start | bytes 2654212 | tf_op jit(solution)/shard_map/cond
  68.9 6.0 %copy-start.14 = (s32[32,896]{1,0:T(8,128)S(1)}, s32[32,896]{1,0:T(8,128)}, u32[]{:S(2)}) copy-start(s32[32,896]{1,0:T(8,128)} %param.24) | copy-start | bytes 344068
  68.9 6.0 %copy-start.15 = (s32[32,896]{1,0:T(8,128)S(1)}, s32[32,896]{1,0:T(8,128)}, u32[]{:S(2)}) copy-start(s32[32,896]{1,0:T(8,128)} %param.23) | copy-start | bytes 344068
  74.4 7.6 %copy-start.1 = (f32[4,32,896]{2,1,0:T(8,128)S(1)}, f32[4,32,896]{2,1,0:T(8,128)}, u32[]{:S(2)}) copy-start(f32[4,32,896]{2,1,0:T(8,128)} %temp.1) | copy-start | bytes 1376260
  74.4 7.6 %copy-start.2 = (s32[32,896]{1,0:T(8,128)S(1)}, s32[32,896]{1,0:T(8,128)}, u32[]{:S(2)}) copy-start(s32[32,896]{1,0:T(8,128)} %mask.1) | copy-start | bytes 344068
  74.9 21.9 %copy-start.8 = (f32[32,24,288]{2,1,0:T(8,128)S(1)}, f32[32,24,288]{2,1,0:T(8,128)}, u32[]{:S(2)}) copy-start(f32[32,24,288]{2,1,0:T(8,128)} %get-tuple-element.105) | copy-start | bytes 2654212
